TPU v7x, 256 devices: a whole 4x4x8 slice. The times are simulated.
256 devices in a mesh: row: 16 (over y, z_hi), col: 16 (over x, z_lo, core).
Axes of the slice: x: 4, y: 4, z: 8 (z_hi: 4, z_lo: 2; z = z_hi * 2 + z_lo), core: 2. Of those that a mesh axis runs over, the one named last changes fastest.
Arguments:
- alignment_left: bfloat16 [1024, 1024], P(('row', 'col')), may hold values from -6 to 6
- alignment_right: bfloat16 [1024, 1024], P(('col', 'row')), may hold values from -6 to 6
- output_weight: bfloat16 [1024, 128], replicated, may hold values from -0.1875 to 0.1875
- bias: float32 [128], replicated, may hold values from -3 to 3
- cotangent: bfloat16 [1024, 1024, 128], P('row', 'col'), may hold values from -6 to 6
Outputs:
- pair: bfloat16 [1024, 1024, 128], P('row', 'col')
- grad_left: bfloat16 [1024, 1024], P(('row', 'col'))
- grad_right: bfloat16 [1024, 1024], P(('col', 'row'))
- grad_w: float32 [1024, 128], P(('row', 'col'))
All inputs are finite; a program needn't handle non-finite values.
Results may differ from a plain program's by a relative error of at most 0.0049.
Values may be sent and summed in bfloat16 or wider, within the bound.
A program may use at most 128 MiB of HBM per device.

v0:
```python
import jax
import jax.numpy as jnp
from jax import lax
from jax.sharding import PartitionSpec as P

LEFT_CHANNELS = 32
RIGHT_CHANNELS = 32
CZ = 128
SEQUENCE_COUNT = 32


def shards(alignment_left, alignment_right, output_weight, bias, cotangent):
    left_input = lax.all_gather(alignment_left, "col", axis=0, tiled=True)
    right_input = lax.all_gather(alignment_right, "row", axis=0, tiled=True)
    rows_i = left_input.shape[0]
    rows_j = right_input.shape[0]
    left_three = left_input.reshape(rows_i, SEQUENCE_COUNT, LEFT_CHANNELS)
    right_three = right_input.reshape(rows_j, SEQUENCE_COUNT, RIGHT_CHANNELS)
    outer = (
        jnp.einsum("isc,jsd->ijcd", left_three, right_three, preferred_element_type=jnp.float32)
        / SEQUENCE_COUNT
    )
    outer = outer.reshape(rows_i * rows_j, LEFT_CHANNELS * RIGHT_CHANNELS).astype(jnp.bfloat16)
    pair = (jnp.dot(outer, output_weight, preferred_element_type=jnp.float32) + bias).astype(
        jnp.bfloat16
    )
    pair = pair.reshape(rows_i, rows_j, CZ)
    g_flat = cotangent.reshape(rows_i * rows_j, CZ)
    g_outer = lax.dot_general(
        g_flat, output_weight, (((1,), (1,)), ((), ())), preferred_element_type=jnp.float32
    )
    g_four = g_outer.astype(jnp.bfloat16).reshape(rows_i, rows_j, LEFT_CHANNELS, RIGHT_CHANNELS)
    left_part = jnp.einsum("ijcd,jsd->isc", g_four, right_three, preferred_element_type=jnp.float32)
    right_part = jnp.einsum("ijcd,isc->jsd", g_four, left_three, preferred_element_type=jnp.float32)
    grad_left = lax.psum_scatter(
        left_part.reshape(rows_i, SEQUENCE_COUNT * LEFT_CHANNELS),
        "col",
        scatter_dimension=0,
        tiled=True,
    )
    grad_right = lax.psum_scatter(
        right_part.reshape(rows_j, SEQUENCE_COUNT * RIGHT_CHANNELS),
        "row",
        scatter_dimension=0,
        tiled=True,
    )
    grad_left = (grad_left / SEQUENCE_COUNT).astype(jnp.bfloat16)
    grad_right = (grad_right / SEQUENCE_COUNT).astype(jnp.bfloat16)
    grad_w = lax.psum_scatter(
        lax.dot_general(
            outer, g_flat, (((0,), (0,)), ((), ())), preferred_element_type=jnp.float32
        ),
        ("row", "col"),
        scatter_dimension=0,
        tiled=True,
    )
    return (pair, grad_left, grad_right, grad_w)


def solution(mesh):
    in_specs = (P(("row", "col"), None), P(("col", "row"), None), P(), P(), P("row", "col", None))
    out_specs = (
        P("row", "col", None),
        P(("row", "col"), None),
        P(("col", "row"), None),
        P(("row", "col"), None),
    )
    return jax.shard_map(shards, mesh=mesh, in_specs=in_specs, out_specs=out_specs, check_vma=False)
```

profile of v0, /device:TPU:1, one launch (start us, length us, event | category | flops | bytes accessed | tf_op | source)
XLA Modules:
  0.0 680.5 jit_solution(10339020405837355308)
XLA Ops:
  7.2 0.0 copy-start
  7.2 0.0 all-reduce.11.cloned.1.call-start
  7.2 22.2 %all-gather.1 = bf16[16,4,1024]{2,1,0:T(4,128)(2,1)S(1)} all-gather(bf16[1,4,1024]{2,1,0:T(4,128)(2,1)} %bitcast.53), channel_id=1, replica_groups=mesh['row'=16,'col'=16] {'col'}, dimensions={0}, use_global_device_ids=true | all-gather | bytes 139264 | tf_op jit(solution)/shard_map/all_gather | solution.py:13
  29.5 39.5 %all-gather = bf16[16,4,1024]{2,1,0:T(4,128)(2,1)S(1)} all-gather(bf16[1,4,1024]{2,1,0:T(4,128)(2,1)} %bitcast.54), channel_id=1, replica_groups=mesh['row'=16,'col'=16] {'row'}, dimensions={0}, use_global_device_ids=true | all-gather | bytes 139264 | tf_op jit(solution)/shard_map/all_gather | solution.py:14
  68.9 0.3 reshape.33
  69.2 0.8 copy.32
  70.0 0.3 reshape.34
  70.3 0.8 copy.23
  71.1 8.1 %fusion = bf16[64,64,32,32]{0,1,2,3:T(8,128)(2,1)} fusion(bf16[64,32,32,1]{0,1,3,2:T(8,128)(2,1)S(1)} %copy.32, bf16[64,32,32]{0,1,2:T(8,128)(2,1)S(1)} %copy.23), kind=kOutput, calls=%fused_computation.1 | convolution fusion | flops 276824064 | bytes 8650752 | tf_op jit(solution)/shard_map/isc,jsd->ijcd/dot_general | solution.py:20
  79.2 22.6 %copy.24 = bf16[64,64,32,32]{1,0,3,2:T(8,128)(2,1)} copy(bf16[64,64,32,32]{0,1,2,3:T(8,128)(2,1)} %fusion) | data formatting | bytes 16777216 | tf_op jit(solution)/shard_map/convert_element_type | solution.py:23
  101.8 0.0 copy-start.1
  101.8 22.6 %convert_element_type.25 = bf16[4096,1024]{0,1:T(8,128)(2,1)} reshape(bf16[64,64,32,32]{1,0,3,2:T(8,128)(2,1)} %copy.24) | data formatting | bytes 16777216 | tf_op jit(solution)/shard_map/convert_element_type | solution.py:23
  124.4 0.0 copy-done
  124.4 6.5 fusion.6
  130.9 0.0 all-reduce.11.cloned.1.call-update
  131.0 0.2 all-reduce.9.cloned.1.call-start
  131.2 0.8 copy.34
  132.0 0.0 copy-done.1
  132.0 5.6 convolution_convert_fusion
  137.6 11.8 %copy.25 = bf16[4096,1024]{0,1:T(8,128)(2,1)} copy(bf16[4096,1024]{1,0:T(8,128)(2,1)} %convolution_convert_fusion) | data formatting | bytes 16777216 | tf_op jit(solution)/shard_map/convert_element_type | solution.py:32
  149.4 23.6 %reshape.37 = bf16[64,64,32,32]{1,0,3,2:T(8,128)(2,1)} reshape(bf16[4096,1024]{0,1:T(8,128)(2,1)} %copy.25) | data formatting | bytes 16777216 | tf_op jit(solution)/shard_map/reshape | solution.py:32
  173.0 0.0 copy-start.2
  173.0 7.4 %convolution_bitcast_fusion = f32[64,32,32]{0,1,2:T(8,128)S(1)} fusion(bf16[64,32,32,1]{0,1,3,2:T(8,128)(2,1)S(1)} %copy.34, bf16[64,64,32,32]{1,0,3,2:T(8,128)(2,1)} %reshape.37), kind=kOutput, calls=%fused_computation.5 | convolution fusion | flops 268435456 | bytes 8781824 | tf_op jit(solution)/shard_map/ijcd,isc->jsd/dot_general | solution.py:34
  180.4 0.0 copy-start.4
  180.4 0.0 copy-start.3
  180.5 1.1 copy.29
  181.6 0.0 all-reduce.9.cloned.1.call-update
  181.6 0.0 all-reduce.7.cloned.1.call-start
  181.7 0.8 copy.26
  182.5 11.0 %convolution_bitcast_fusion.1 = f32[64,32,32]{0,1,2:T(8,128)S(1)} fusion(bf16[64,64,32,32]{1,0,3,2:T(8,128)(2,1)} %reshape.37, bf16[64,32,32]{0,1,2:T(8,128)(2,1)S(1)} %copy.26), kind=kOutput, calls=%fused_computation.6 | convolution fusion | flops 268435456 | bytes 8781824 | tf_op jit(solution)/shard_map/ijcd,jsd->isc/dot_general | solution.py:33
  193.4 1.1 copy.27
  194.6 0.0 all-reduce.7.cloned.1.call-update
  194.6 0.0 copy-done.2
  194.6 6.8 fusion.1
  201.3 0.0 copy-done.4
  201.3 0.6 dynamic-slice.2
  202.6 0.0 copy-done.3
  202.6 0.6 dynamic-slice
  203.8 175.6 %all-reduce.11.cloned.1.call-done = f32[1024,128]{1,0:T(8,128)} async-done(((f32[1024,128]{1,0:T(8,128)}), f32[1024,128]{1,0:T(8,128)}) %all-reduce.11.cloned.1.call-update) | async-done | bytes 524304
  379.4 1.3 constant_dynamic-slice_fusion
  380.7 158.4 %all-reduce.9.cloned.1.call-done = f32[64,1024]{0,1:T(8,128)} async-done(((f32[64,1024]{0,1:T(8,128)}), f32[64,1024]{0,1:T(8,128)}) %all-reduce.9.cloned.1.call-update) | async-done | bytes 262160
  539.1 1.2 fusion.2
  540.4 0.7 copy.31
  541.1 130.9 %all-reduce.7.cloned.1.call-done = f32[64,1024]{0,1:T(8,128)} async-done(((f32[64,1024]{0,1:T(8,128)}), f32[64,1024]{0,1:T(8,128)}) %all-reduce.7.cloned.1.call-update) | async-done | bytes 262160
  672.0 1.2 fusion.3
  673.2 0.7 copy.30
Async XLA Ops:
  7.2 117.2 %copy-start = (bf16[64,64,128]{2,1,0:T(8,128)(2,1)S(1)}, bf16[64,64,128]{2,1,0:T(8,128)(2,1)}, u32[]{:S(2)}) copy-start(bf16[64,64,128]{2,1,0:T(8,128)(2,1)} %param.9) | copy-start | bytes 3145732
  7.2 372.2 %all-reduce.11.cloned.1.call-start = ((), (), s32[]{:S(2)}) async-start(), calls=%async_computation.2 | async-start | bytes 1048576
  101.8 30.2 %copy-start.1 = (bf16[1024,128]{1,0:T(8,128)(2,1)S(1)}, bf16[1024,128]{1,0:T(8,128)(2,1)}, u32[]{:S(2)}) copy-start(bf16[1024,128]{1,0:T(8,128)(2,1)} %param.7) | copy-start | bytes 786436
  131.0 408.2 %all-reduce.9.cloned.1.call-start = ((), (), s32[]{:S(2)}) async-start(), calls=%async_computation.1 | async-start | bytes 1048576
  173.0 21.6 %copy-start.2 = (f32[128]{0:T(128)S(1)}, f32[128]{0:T(128)}, u32[]{:S(2)}) copy-start(f32[128]{0:T(128)} %param.8) | copy-start | bytes 1540
  180.4 20.9 %copy-start.4 = (u32[256]{0:T(256)S(1)}, u32[256]{0:T(256)}, u32[]{:S(2)}) copy-start(u32[256]{0:T(256)} %constant.14) | copy-start | bytes 3076
  180.4 22.1 %copy-start.3 = (u32[256]{0:T(256)S(1)}, u32[256]{0:T(256)}, u32[]{:S(2)}) copy-start(u32[256]{0:T(256)} %constant.10) | copy-start | bytes 3076
  181.6 490.4 %all-reduce.7.cloned.1.call-start = ((), (), s32[]{:S(2)}) async-start(), calls=%async_computation | async-start | bytes 1048576
Sparse Core Ops, SparseCore 0:
  131.1 248.2 all-reduce.10
  382.0 157.0 all-reduce.8
  541.9 130.0 all-reduce.6
where the time goes:
time: 683 us; the launch traced here: 680 us
  waiting for transfers between devices  465 us (68%)
  local copies, waits for them, and re-layouts  90.5 us (13%)
  blocking collectives  61.7 us (9%)
  matrix products  45.4 us (7%)
  between operations  15.2 us (2%)
    unnamed x6, waiting for transfers between devices  465 us
    convert_element_type x2, local copies, waits for them, and re-layouts, shards(): outer.reshape(rows_i * rows_j, LEFT_CHANNELS * RIGHT_CHANNELS)  45.2 us
    all_gather x1, blocking collectives, shards(): right_input = lax.all_gather(alignment_right, 'row', axis=0, tiled=True)  39.5 us
    reshape x1, local copies, waits for them, and re-layouts, shards(): g_outer.astype(jnp.bfloat16)  23.6 us
    all_gather x1, blocking collectives, shards(): left_input = lax.all_gather(alignment_left, 'col', axis=0, tiled=True)  22.2 us
  transfers between devices with their start and end apart: 3, of which 3 were waited for; matrix products, arithmetic and copies ran while one was open for 11% of the time, Pallas kernels for 0%

commit v1 on v0

v1 whole, which is shorter than its diff:
```python
import functools

import jax
import jax.numpy as jnp
from jax import lax
from jax.experimental import pallas as pl
from jax.experimental.pallas import tpu as pltpu
from jax.sharding import PartitionSpec as P

MESH = pl.DeviceIdType.MESH
BF, F32 = jnp.bfloat16, jnp.float32
S, C, D, Z = 32, 32, 32, 128
N = 16
L = 4
R = N * L
SCALE = 1.0 / S


def dot(a, b):
    return jnp.dot(a, b, preferred_element_type=F32)


def iota(shape, dim):
    return lax.broadcasted_iota(jnp.int32, shape, dim)


def kernel(
    a_ref, b_ref, w_ref, bias_ref, x_hbm, pair_hbm, gl_ref, gr_ref, gw_ref,
    x, xt, wp, wpt, w32, mask, g, o, arep, arept, bp, bpt, b32, bs32,
    gw, gwt, gr, gs32, pairv,
    a_all, b_all, w1_out, w1_in, w2_out, w2_in, l_out, l_in, r_out, r_in,
    x_sem, p_sem, send, recv,
):
    row, col = lax.axis_index("row"), lax.axis_index("col")

    def on_col(k):
        return (row, k)

    def on_row(k):
        return (k, col)

    def push(src, dst, which, device):
        pltpu.make_async_remote_copy(
            src_ref=src, dst_ref=dst, send_sem=send.at[which], recv_sem=recv.at[which],
            device_id=device, device_id_type=MESH,
        ).start()

    def others(me, body):
        def step(t, carry):
            body(lax.rem(me + t, N))
            return carry

        lax.fori_loop(1, N, step, 0)

    def wait_all(ref, sem):
        blocks = ref.at[pl.ds(0, N - 1)]
        pltpu.make_async_copy(blocks, blocks, sem).wait()

    A, B, W1, W2, GL, GR = range(6)

    barrier = pltpu.get_barrier_semaphore()

    def greet(k, to):
        pl.semaphore_signal(barrier, inc=1, device_id=to(k), device_id_type=MESH)

    others(col, lambda k: greet(k, on_col))
    others(row, lambda k: greet(k, on_row))

    def x_load(q):
        part = pl.ds(q * 16, 16)
        return pltpu.make_async_copy(x_hbm.at[part], x.at[part], x_sem.at[q])

    for q in range(4):
        x_load(q).start()
    a_all[col] = a_ref[...]
    b_all[row] = b_ref[...]

    pl.semaphore_wait(barrier, 2 * (N - 1))
    others(row, lambda k: push(b_ref, b_all.at[row], B, on_row(k)))
    others(col, lambda k: push(a_ref, a_all.at[col], A, on_col(k)))

    w32[...] = w_ref[...].astype(F32)
    for d in range(D):
        wp[pl.ds(d * C, C), :] = w32[pl.ds(d, C, stride=D), :].astype(BF)
    for q in range(8):
        wpt[:, pl.ds(q * 128, 128)] = wp[pl.ds(q * 128, 128), :].T
    mask[...] = (iota((256, 256), 0) // 32 == iota((256, 256), 1) // 32).astype(F32).astype(BF)

    for q in range(4):
        x_load(q).wait()

    def outer_grad(q, carry):
        rows = x[pl.ds(q * 8, 8)].reshape(8 * R, Z)
        for dh in range(4):
            part = dot(rows, wpt[:, pl.ds(dh * 256, 256)]).astype(BF)
            g[pl.ds(q * 8, 8), pl.ds(dh * R, R), :] = part.reshape(8, R, 256)
        return carry

    lax.fori_loop(0, 8, outer_grad, 0)

    def x_transpose(q, carry):
        for h in range(4):
            rows = x[pl.ds(q * 16 + h * 4, 4)].reshape(256, Z)
            xt[q, :, pl.ds(h * 256, 256)] = rows.T
        return carry

    lax.fori_loop(0, 4, x_transpose, 0)

    wait_all(b_all, recv.at[B])
    wait_all(a_all, recv.at[A])
    bs32[...] = b_all[...].astype(F32)
    for q in range(N):
        for dh in range(4):
            b32[pl.ds(dh * R + q * L, L), :] = bs32[q, pl.ds(dh * L, L), :]
    bp[...] = b32[...].astype(BF)
    bpt[...] = b32[...].T.astype(BF)

    spread = jnp.where(
        (iota((128, 1024), 0) // 32 == iota((128, 1024), 1) // 256)
        & (iota((128, 1024), 0) % 32 == iota((128, 1024), 1) % 32), SCALE, 0.0).astype(BF)
    arep[...] = dot(a_all[...].reshape(N * S, 128), spread).astype(BF).reshape(N, S, 1024)
    spread_t = jnp.where(iota((32, 256), 0) == iota((32, 256), 1) % 32, SCALE, 0.0).astype(BF)

    def transposed(q, carry):
        arept[q] = dot(a_all[q].astype(F32).T.astype(BF), spread_t).astype(BF)
        return carry

    lax.fori_loop(0, N, transposed, 0)

    def diagonal(block):
        return jnp.concatenate([block] * 8, axis=0) * mask[...]

    def outer(q, carry):
        for i in range(L):
            o[q * L + i] = dot(bp[...], diagonal(arep[q, :, pl.ds(i * 256, 256)])).astype(BF)
        return carry

    lax.fori_loop(0, N, outer, 0)

    for q in range(4):
        for dh in range(4):
            rows = o[pl.ds(q * 16, 16), pl.ds(dh * R, R), :].reshape(16 * R, 256)
            part = dot(xt[q], rows)
            if q == 0:
                gw[:, pl.ds(dh * 256, 256)] = part
            else:
                gw[:, pl.ds(dh * 256, 256)] += part
    for q in range(8):
        gwt[pl.ds(q * 128, 128), :] = gw[:, pl.ds(q * 128, 128)].T
    for k in range(N):
        for dl in range(4):
            first = (4 * (k % 8) + dl) * C + k // 8
            w1_out[k, pl.ds(dl * 16, 16), :] = gwt[pl.ds(first, 16, stride=2), :].astype(BF)
    w1_in[col] = w1_out[col]
    others(col, lambda k: push(w1_out.at[k], w1_in.at[col], W1, on_col(k)))

    gr[...] = jnp.zeros_like(gr)

    def right_grad(q, carry):
        total = gr[...]
        for i in range(L):
            total += dot(g[q * L + i], diagonal(arept[q, pl.ds(i * 32, 32), :]))
        gr[...] = total
        return carry

    lax.fori_loop(0, N, right_grad, 0)
    for q in range(N):
        for dh in range(4):
            gs32[q, pl.ds(dh * L, L), :] = gr[pl.ds(dh * R + q * L, L), :]
    r_out[...] = gs32[...].astype(BF)
    r_in[row] = r_out[row]
    others(row, lambda k: push(r_out.at[k], r_in.at[row], GR, on_row(k)))

    lane4 = iota((32, 256), 1) % 128 // 32
    lane = iota((32, 128), 1) // 32

    def left_group(q):
        result = jnp.zeros((32, 128), F32)
        for pair in range(2):
            i0 = q * L + pair * 2
            both = jnp.zeros((32, 256), F32)
            for h in range(2):
                half = pl.ds(h * 128, 128)
                rhs = jnp.concatenate([g[i0, :, half], g[i0 + 1, :, half]], axis=1)
                part = dot(bpt[half, :], rhs)
                kept = part[96:128]
                for dl in range(3):
                    kept = jnp.where(lane4 == dl, part[dl * 32 : dl * 32 + 32], kept)
                both += kept
            for i in range(2):
                one = both[:, i * 128 : i * 128 + 128]
                one = one + pltpu.roll(one, 64, 1)
                one = one + pltpu.roll(one, 32, 1)
                result = jnp.where(lane == pair * 2 + i, one, result)
        l_out[q] = result.astype(BF)

    def left_step(t, carry):
        q = lax.rem(col + t, N)
        left_group(q)
        push(l_out.at[q], l_in.at[col], GL, on_col(q))
        return carry

    lax.fori_loop(1, N, left_step, 0)
    left_group(col)
    l_in[col] = l_out[col]

    wait_all(w1_in, recv.at[W1])
    total = w1_in[0].astype(F32)
    for k in range(1, N):
        total += w1_in[k].astype(F32)
    gwt[pl.ds(0, 64), :] = total
    for k in range(N):
        w2_out[k] = jnp.concatenate([gwt[pl.ds(k, 4, stride=16), :]] * 2, axis=0)
    w2_in[row] = w2_out[row]
    others(row, lambda k: push(w2_out.at[k], w2_in.at[row], W2, on_row(k)))

    def pair_store(q):
        part = pl.ds(q * 8, 8)
        return pltpu.make_async_copy(pairv.at[part], pair_hbm.at[part], p_sem.at[q])

    def pair_block(q, carry):
        total = jnp.broadcast_to(bias_ref[...], (8 * R, Z))
        for dh in range(4):
            rows = o[pl.ds(q * 8, 8), pl.ds(dh * R, R), :].reshape(8 * R, 256)
            total += dot(rows, wp[pl.ds(dh * 256, 256), :])
        pairv[pl.ds(q * 8, 8)] = total.astype(BF).reshape(8, R, Z)
        pair_store(q).start()
        return carry

    lax.fori_loop(0, 8, pair_block, 0)

    wait_all(r_in, recv.at[GR])
    total = r_in[0].astype(F32)
    for k in range(1, N):
        total += r_in[k].astype(F32)
    gr_ref[...] = total.astype(BF)
    wait_all(l_in, recv.at[GL])
    total = l_in[0].astype(F32)
    for k in range(1, N):
        total += l_in[k].astype(F32)
    gl_ref[...] = (total * SCALE).astype(BF)
    wait_all(w2_in, recv.at[W2])
    total = w2_in[0]
    for k in range(1, N):
        total += w2_in[k]
    gw_ref[...] = total[0:4]

    for ref, which in ((a_all, A), (b_all, B), (w1_in, W1), (w2_in, W2), (l_in, GL), (r_in, GR)):
        wait_all(ref, send.at[which])

    def drain(q, carry):
        pair_store(q).wait()
        return carry

    lax.fori_loop(0, 8, drain, 0)


def shards(a, b, w, bias, x):
    a = a.reshape(L, S, C).transpose(1, 0, 2).reshape(S, L * C)
    b = b.reshape(L, S, 4, 8).transpose(2, 0, 3, 1).reshape(4 * L, 8 * S)
    vmem = pl.BlockSpec(memory_space=pltpu.VMEM)
    hbm = pl.BlockSpec(memory_space=pl.ANY)
    v = pltpu.VMEM
    pair, gl, gr, gw = pl.pallas_call(
        kernel,
        out_shape=(
            jax.ShapeDtypeStruct((R, R, Z), BF),
            jax.ShapeDtypeStruct((S, L * C), BF),
            jax.ShapeDtypeStruct((4 * L, 8 * S), BF),
            jax.ShapeDtypeStruct((4, Z), F32),
        ),
        in_specs=[vmem, vmem, vmem, vmem, hbm],
        out_specs=(hbm, vmem, vmem, vmem),
        scratch_shapes=[
            v((R, R, Z), BF), v((4, Z, 1024), BF), v((1024, Z), BF), v((Z, 1024), BF), v((1024, Z), F32),
            v((256, 256), BF), v((R, 256, 256), BF), v((R, 256, 256), BF),
            v((N, S, 1024), BF), v((N, 128, 256), BF),
            v((256, 256), BF), v((256, 256), BF), v((256, 256), F32), v((N, 16, 256), F32),
            v((Z, 1024), F32), v((1024, Z), F32), v((256, 256), F32), v((N, 16, 256), F32),
            v((R, R, Z), BF),
            v((N, S, 128), BF), v((N, 16, 256), BF),
            v((N, 64, Z), BF), v((N, 64, Z), BF), v((N, 8, Z), F32), v((N, 8, Z), F32),
            v((N, S, 128), BF), v((N, S, 128), BF), v((N, 16, 256), BF), v((N, 16, 256), BF),
            pltpu.SemaphoreType.DMA((4,)), pltpu.SemaphoreType.DMA((8,)),
            pltpu.SemaphoreType.DMA((6,)), pltpu.SemaphoreType.DMA((6,)),
        ],
        compiler_params=pltpu.CompilerParams(
            collective_id=0, has_side_effects=True, vmem_limit_bytes=48 * 2**20
        ),
        cost_estimate=pl.CostEstimate(
            flops=8_000_000_000, bytes_accessed=3_000_000, transcendentals=0
        ),
    )(a, b, w, bias.reshape(1, Z), x)
    gl = gl.reshape(S, L, C).transpose(1, 0, 2).reshape(L, S * C)
    gr = gr.reshape(4, L, 8, S).transpose(1, 3, 0, 2).reshape(L, S * D)
    return pair, gl, gr, gw


def solution(mesh):
    in_specs = (P(("row", "col"), None), P(("col", "row"), None), P(), P(), P("row", "col", None))
    out_specs = (
        P("row", "col", None),
        P(("row", "col"), None),
        P(("col", "row"), None),
        P(("row", "col"), None),
    )
    return jax.shard_map(shards, mesh=mesh, in_specs=in_specs, out_specs=out_specs, check_vma=False)
```

time: 683 us -> 54 us (0.08)
  waiting for transfers between devices: 465 us -> 0 us
  local copies, waits for them, and re-layouts: 90.5 us -> 7.18 us
  blocking collectives: 61.7 us -> 0 us
  Pallas kernels: 0 us -> 45.9 us
  matrix products: 45.4 us -> 0 us
  between operations: 15.2 us -> 0.7 us
    unnamed x6 -> x0, waiting for transfers between devices: 465 us -> none
    all_gather x2 -> x0, blocking collectives: 61.7 us -> none  [the longest x1 39.5 us: shards(): right_input = lax.all_gather(alignment_right, 'row', axis=0, tiled=True)]
    convert_element_type x3 -> x0, local copies, waits for them, and re-layouts: 57 us -> none  [the longest x2 45.2 us: shards(): outer.reshape(rows_i * rows_j, LEFT_CHANNELS * RIGHT_CHANNELS)]
    pallas_call x0 -> x1, Pallas kernels: none -> 45.9 us  [shards(): pl.pallas_call(kernel, out_shape=(jax.ShapeDtypeStruct((R, R, Z), BF), ja...]
    dot_general x6 -> x0, matrix products: 45.4 us -> none  [the longest x1 11 us: shards(): jnp.einsum('ijcd,jsd->isc', g_four, right_three, preferred_element_type=j...]
    reshape x7 -> x10, local copies, waits for them, and re-layouts: 27.3 us -> 3.71 us  [the longest x3 1 us: shards(): gr = gr.reshape(4, L, 8, S).transpose(1, 3, 0, 2).reshape(L, S * D)]
  transfers between devices with their start and end apart: 3 -> 0, of which waited for: 3 -> 0; matrix products, arithmetic and copies ran while one was open for 11% -> 0% of each run, Pallas kernels for 0% -> 0%
where the time goes in v1:
time: 54 us; the launch traced here: 53.8 us
  Pallas kernels  45.9 us (85%)
  local copies, waits for them, and re-layouts  7.18 us (13%)
  between operations  0.7 us (1%)
    pallas_call x1, Pallas kernels, shards(): pl.pallas_call(kernel, out_shape=(jax.ShapeDtypeStruct((R, R, Z), BF), ja...  45.9 us
    unnamed x8, local copies, waits for them, and re-layouts  3.33 us

profile of v1, /device:TPU:1, one launch (start us, length us, event | category | flops | bytes accessed | tf_op | source)
XLA Modules:
  0.0 53.8 jit_solution(2651202719916205485)
XLA Ops:
  0.6 0.0 copy-start.1
  0.6 0.8 %reshape.35 = bf16[4,32,32]{2,1,0:T(8,128)(2,1)S(1)} reshape(bf16[4,1024]{1,0:T(4,128)(2,1)} %param.5) | data formatting | bytes 16384 | tf_op jit(solution)/shard_map/reshape | solution.py:259
  1.5 0.1 reshape.36.a_ref
  1.6 0.9 %reshape.37 = bf16[4,32,4,8]{3,2,1,0:T(4,128)(2,1)S(1)} reshape(bf16[4,1024]{1,0:T(4,128)(2,1)} %param.6) | data formatting | bytes 16384 | tf_op jit(solution)/shard_map/reshape | solution.py:260
  2.5 0.1 copy.14
  2.6 0.0 copy-start.2
  2.6 0.1 reshape.38.b_ref
  2.7 0.0 copy-done.1
  2.7 0.6 %copy-done.2 = f32[128]{0:T(128)S(1)} copy-done((f32[128]{0:T(128)S(1)}, f32[128]{0:T(128)}, u32[]{:S(2)}) %copy-start.2) | copy-done | bytes 536
  3.3 0.0 copy-start
  3.3 1.2 %copy-done = bf16[64,64,128]{2,1,0:T(8,128)(2,1)S(1)} copy-done((bf16[64,64,128]{2,1,0:T(8,128)(2,1)S(1)}, bf16[64,64,128]{2,1,0:T(8,128)(2,1)}, u32[]{:S(2)}) %copy-start) | copy-done | bytes 1048600
  4.5 45.9 %shard_map.84 = (bf16[64,64,128]{2,1,0:T(8,128)(2,1)S(1)}, bf16[32,128]{1,0:T(8,128)(2,1)S(1)}, bf16[16,256]{1,0:T(8,128)(2,1)S(1)}, f32[4,128]{1,0:T(4,128)S(1)}) custom-call(bf16[32,128]{1,0:T(8,128)(2,1)S(1)} %reshape.36.a_ref, bf16[16,256]{1,0:T(8,128)(2,1)S(1)} %reshape.38.b_ref, bf16[1024,128]{1,0:T(8,128)(2,1)S(1)} %copy-done.1, ...), custom_call_target="tpu_custom_call" | custom-call | flops 8000000000 | bytes 3000000 | tf_op jit(solution)/shard_map/pallas_call | solution.py:264
  50.5 0.1 reshape.40
  50.6 0.7 %reshape.41 = bf16[4,1024]{1,0:T(4,128)(2,1)} reshape(bf16[4,32,32]{2,1,0:T(8,128)(2,1)S(1)} %copy.15) | data formatting | bytes 16384 | tf_op jit(solution)/shard_map/reshape | solution.py:294
  51.3 0.1 reshape.42
  51.3 0.1 copy.16
  51.5 0.8 %reshape.43 = bf16[4,1024]{1,0:T(4,128)(2,1)} reshape(bf16[4,32,4,8]{3,2,1,0:T(4,128)(2,1)S(1)} %bitcast.10) | data formatting | bytes 16384 | tf_op jit(solution)/shard_map/reshape | solution.py:295
  52.3 1.0 %copy.21 = bf16[64,64,128]{2,1,0:T(8,128)(2,1)} copy(bf16[64,64,128]{2,1,0:T(8,128)(2,1)S(1)} %get-tuple-element.16) | data formatting | bytes 2097152
  53.2 0.6 %copy.22 = f32[4,128]{1,0:T(4,128)} copy(f32[4,128]{1,0:T(4,128)S(1)} %get-tuple-element.19) | data formatting | bytes 4096
  (2 shorter events, 0.0 us)
Async XLA Ops:
  0.6 2.1 %copy-start.1 = (bf16[1024,128]{1,0:T(8,128)(2,1)S(1)}, bf16[1024,128]{1,0:T(8,128)(2,1)}, u32[]{:S(2)}) copy-start(bf16[1024,128]{1,0:T(8,128)(2,1)} %w_ref.1) | copy-start | bytes 786436
  2.6 0.7 %copy-start.2 = (f32[128]{0:T(128)S(1)}, f32[128]{0:T(128)}, u32[]{:S(2)}) copy-start(f32[128]{0:T(128)} %param.8) | copy-start | bytes 1540
  3.3 1.2 %copy-start = (bf16[64,64,128]{2,1,0:T(8,128)(2,1)S(1)}, bf16[64,64,128]{2,1,0:T(8,128)(2,1)}, u32[]{:S(2)}) copy-start(bf16[64,64,128]{2,1,0:T(8,128)(2,1)} %x_hbm.1) | copy-start | bytes 3145732

commit v2 on v1

--- a/solution.py
+++ b/solution.py
@@ -90,13 +90,13 @@
         x_load(q).wait()
 
     def outer_grad(q, carry):
-        rows = x[pl.ds(q * 8, 8)].reshape(8 * R, Z)
+        rows = x[pl.ds(q * 16, 16)].reshape(16 * R, Z)
+        part = dot(rows, wpt[...]).astype(BF)
         for dh in range(4):
-            part = dot(rows, wpt[:, pl.ds(dh * 256, 256)]).astype(BF)
-            g[pl.ds(q * 8, 8), pl.ds(dh * R, R), :] = part.reshape(8, R, 256)
-        return carry
-
-    lax.fori_loop(0, 8, outer_grad, 0)
+            g[pl.ds(q * 16, 16), pl.ds(dh * R, R), :] = part[:, dh * 256 : dh * 256 + 256].reshape(16, R, 256)
+        return carry
+
+    lax.fori_loop(0, 4, outer_grad, 0)
 
     def x_transpose(q, carry):
         for h in range(4):
@@ -119,23 +119,21 @@
         (iota((128, 1024), 0) // 32 == iota((128, 1024), 1) // 256)
         & (iota((128, 1024), 0) % 32 == iota((128, 1024), 1) % 32), SCALE, 0.0).astype(BF)
     arep[...] = dot(a_all[...].reshape(N * S, 128), spread).astype(BF).reshape(N, S, 1024)
-    spread_t = jnp.where(iota((32, 256), 0) == iota((32, 256), 1) % 32, SCALE, 0.0).astype(BF)
-
-    def transposed(q, carry):
-        arept[q] = dot(a_all[q].astype(F32).T.astype(BF), spread_t).astype(BF)
-        return carry
-
-    lax.fori_loop(0, N, transposed, 0)
+    for q in range(4):
+        turned = a_all[pl.ds(q * 4, 4)].reshape(128, 128).T
+        arept[q] = dot(turned, spread).astype(BF)
 
     def diagonal(block):
         return jnp.concatenate([block] * 8, axis=0) * mask[...]
 
     def outer(q, carry):
-        for i in range(L):
-            o[q * L + i] = dot(bp[...], diagonal(arep[q, :, pl.ds(i * 256, 256)])).astype(BF)
-        return carry
-
-    lax.fori_loop(0, N, outer, 0)
+        for t in range(4):
+            for i in range(L):
+                rhs = diagonal(arep[q * 4 + t, :, pl.ds(i * 256, 256)])
+                o[q * 16 + t * 4 + i] = dot(bp[...], rhs).astype(BF)
+        return carry
+
+    lax.fori_loop(0, 4, outer, 0)
 
     for q in range(4):
         for dh in range(4):
@@ -157,13 +155,14 @@
     gr[...] = jnp.zeros_like(gr)
 
     def right_grad(q, carry):
-        total = gr[...]
-        for i in range(L):
-            total += dot(g[q * L + i], diagonal(arept[q, pl.ds(i * 32, 32), :]))
-        gr[...] = total
-        return carry
-
-    lax.fori_loop(0, N, right_grad, 0)
+        lhs = jnp.concatenate([g[q * 16 + i] for i in range(16)], axis=1)
+        rhs = jnp.concatenate(
+            [diagonal(arept[q, pl.ds(i % 4 * 32, 32), pl.ds(i // 4 * 256, 256)]) for i in range(16)], axis=0
+        )
+        gr[...] += dot(lhs, rhs)
+        return carry
+
+    lax.fori_loop(0, 4, right_grad, 0)
     for q in range(N):
         for dh in range(4):
             gs32[q, pl.ds(dh * L, L), :] = gr[pl.ds(dh * R + q * L, L), :]
@@ -194,14 +193,20 @@
                 result = jnp.where(lane == pair * 2 + i, one, result)
         l_out[q] = result.astype(BF)
 
-    def left_step(t, carry):
-        q = lax.rem(col + t, N)
-        left_group(q)
-        push(l_out.at[q], l_in.at[col], GL, on_col(q))
-        return carry
-
-    lax.fori_loop(1, N, left_step, 0)
-    left_group(col)
+    def left_step(u, carry):
+        for v in range(4):
+            left_group(lax.rem(col + 4 * u + v + 1, N))
+        for v in range(4):
+            t = 4 * u + v + 1
+            q = lax.rem(col + t, N)
+
+            @pl.when(t < N)
+            def _():
+                push(l_out.at[q], l_in.at[col], GL, on_col(q))
+
+        return carry
+
+    lax.fori_loop(0, 4, left_step, 0)
     l_in[col] = l_out[col]
 
     wait_all(w1_in, recv.at[W1])
@@ -218,16 +223,14 @@
         part = pl.ds(q * 8, 8)
         return pltpu.make_async_copy(pairv.at[part], pair_hbm.at[part], p_sem.at[q])
 
-    def pair_block(q, carry):
-        total = jnp.broadcast_to(bias_ref[...], (8 * R, Z))
-        for dh in range(4):
-            rows = o[pl.ds(q * 8, 8), pl.ds(dh * R, R), :].reshape(8 * R, 256)
-            total += dot(rows, wp[pl.ds(dh * 256, 256), :])
-        pairv[pl.ds(q * 8, 8)] = total.astype(BF).reshape(8, R, Z)
-        pair_store(q).start()
-        return carry
-
-    lax.fori_loop(0, 8, pair_block, 0)
+    for q in range(16):
+        lhs = jnp.concatenate(
+            [o[pl.ds(q * 4, 4), pl.ds(dh * R, R), :].reshape(4 * R, 256) for dh in range(4)], axis=1
+        )
+        total = dot(lhs, wp[...]) + bias_ref[...]
+        pairv[pl.ds(q * 4, 4)] = total.astype(BF).reshape(4, R, Z)
+        if q % 2:
+            pair_store(q // 2).start()
 
     wait_all(r_in, recv.at[GR])
     total = r_in[0].astype(F32)
@@ -274,7 +277,7 @@
         scratch_shapes=[
             v((R, R, Z), BF), v((4, Z, 1024), BF), v((1024, Z), BF), v((Z, 1024), BF), v((1024, Z), F32),
             v((256, 256), BF), v((R, 256, 256), BF), v((R, 256, 256), BF),
-            v((N, S, 1024), BF), v((N, 128, 256), BF),
+            v((N, S, 1024), BF), v((4, 128, 1024), BF),
             v((256, 256), BF), v((256, 256), BF), v((256, 256), F32), v((N, 16, 256), F32),
             v((Z, 1024), F32), v((1024, Z), F32), v((256, 256), F32), v((N, 16, 256), F32),
             v((R, R, Z), BF),

time: 54 us -> 44.1 us (0.82)
  Pallas kernels: 45.9 us -> 36.1 us
    pallas_call x1, Pallas kernels: 45.9 us -> 36.1 us  [shards(): pl.pallas_call(kernel, out_shape=(jax.ShapeDtypeStruct((R, R, Z), BF), ja...]
where the time goes in v2:
time: 44.1 us; the launch traced here: 43.9 us
  Pallas kernels  36.1 us (82%)
  local copies, waits for them, and re-layouts  7.18 us (16%)
  between operations  0.7 us (2%)
    pallas_call x1, Pallas kernels, shards(): pl.pallas_call(kernel, out_shape=(jax.ShapeDtypeStruct((R, R, Z), BF), ja...  36.1 us
    unnamed x8, local copies, waits for them, and re-layouts  3.33 us
    reshape x3, local copies, waits for them, and re-layouts, shards(): gr = gr.reshape(4, L, 8, S).transpose(1, 3, 0, 2).reshape(L, S * D)  1 us
    reshape x2, local copies, waits for them, and re-layouts, shards(): b = b.reshape(L, S, 4, 8).transpose(2, 0, 3, 1).reshape(4 * L, 8 * S)  0.98 us
    reshape x3, local copies, waits for them, and re-layouts, shards(): a = a.reshape(L, S, C).transpose(1, 0, 2).reshape(S, L * C)  0.94 us

profile of v2, /device:TPU:1, one launch (start us, length us, event | category | flops | bytes accessed | tf_op | source)
XLA Modules:
  0.0 43.9 jit_solution(10572437346520123259)
XLA Ops:
  0.6 0.0 copy-start.1
  0.6 0.8 %reshape.35 = bf16[4,32,32]{2,1,0:T(8,128)(2,1)S(1)} reshape(bf16[4,1024]{1,0:T(4,128)(2,1)} %param.5) | data formatting | bytes 16384 | tf_op jit(solution)/shard_map/reshape | solution.py:262
  1.5 0.1 reshape.36.a_ref
  1.6 0.9 %reshape.37 = bf16[4,32,4,8]{3,2,1,0:T(4,128)(2,1)S(1)} reshape(bf16[4,1024]{1,0:T(4,128)(2,1)} %param.6) | data formatting | bytes 16384 | tf_op jit(solution)/shard_map/reshape | solution.py:263
  2.5 0.1 copy.14
  2.6 0.0 copy-start.2
  2.6 0.1 reshape.38.b_ref
  2.7 0.0 copy-done.1
  2.7 0.6 %copy-done.2 = f32[128]{0:T(128)S(1)} copy-done((f32[128]{0:T(128)S(1)}, f32[128]{0:T(128)}, u32[]{:S(2)}) %copy-start.2) | copy-done | bytes 536
  3.3 0.0 copy-start
  3.3 1.2 %copy-done = bf16[64,64,128]{2,1,0:T(8,128)(2,1)S(1)} copy-done((bf16[64,64,128]{2,1,0:T(8,128)(2,1)S(1)}, bf16[64,64,128]{2,1,0:T(8,128)(2,1)}, u32[]{:S(2)}) %copy-start) | copy-done | bytes 1048600
  4.5 36.1 %shard_map.84 = (bf16[64,64,128]{2,1,0:T(8,128)(2,1)S(1)}, bf16[32,128]{1,0:T(8,128)(2,1)S(1)}, bf16[16,256]{1,0:T(8,128)(2,1)S(1)}, f32[4,128]{1,0:T(4,128)S(1)}) custom-call(bf16[32,128]{1,0:T(8,128)(2,1)S(1)} %reshape.36.a_ref, bf16[16,256]{1,0:T(8,128)(2,1)S(1)} %reshape.38.b_ref, bf16[1024,128]{1,0:T(8,128)(2,1)S(1)} %copy-done.1, ...), custom_call_target="tpu_custom_call" | custom-call | flops 8000000000 | bytes 3000000 | tf_op jit(solution)/shard_map/pallas_call | solution.py:267
  40.6 0.1 reshape.40
  40.7 0.7 %reshape.41 = bf16[4,1024]{1,0:T(4,128)(2,1)} reshape(bf16[4,32,32]{2,1,0:T(8,128)(2,1)S(1)} %copy.15) | data formatting | bytes 16384 | tf_op jit(solution)/shard_map/reshape | solution.py:297
  41.4 0.1 reshape.42
  41.5 0.1 copy.16
  41.6 0.8 %reshape.43 = bf16[4,1024]{1,0:T(4,128)(2,1)} reshape(bf16[4,32,4,8]{3,2,1,0:T(4,128)(2,1)S(1)} %bitcast.10) | data formatting | bytes 16384 | tf_op jit(solution)/shard_map/reshape | solution.py:298
  42.4 1.0 %copy.21 = bf16[64,64,128]{2,1,0:T(8,128)(2,1)} copy(bf16[64,64,128]{2,1,0:T(8,128)(2,1)S(1)} %get-tuple-element.16) | data formatting | bytes 2097152
  43.4 0.6 %copy.22 = f32[4,128]{1,0:T(4,128)} copy(f32[4,128]{1,0:T(4,128)S(1)} %get-tuple-element.19) | data formatting | bytes 4096
  (2 shorter events, 0.0 us)
Async XLA Ops:
  0.6 2.1 %copy-start.1 = (bf16[1024,128]{1,0:T(8,128)(2,1)S(1)}, bf16[1024,128]{1,0:T(8,128)(2,1)}, u32[]{:S(2)}) copy-start(bf16[1024,128]{1,0:T(8,128)(2,1)} %w_ref.1) | copy-start | bytes 786436
  2.6 0.7 %copy-start.2 = (f32[128]{0:T(128)S(1)}, f32[128]{0:T(128)}, u32[]{:S(2)}) copy-start(f32[128]{0:T(128)} %param.8) | copy-start | bytes 1540
  3.3 1.2 %copy-start = (bf16[64,64,128]{2,1,0:T(8,128)(2,1)S(1)}, bf16[64,64,128]{2,1,0:T(8,128)(2,1)}, u32[]{:S(2)}) copy-start(bf16[64,64,128]{2,1,0:T(8,128)(2,1)} %x_hbm.1) | copy-start | bytes 3145732

commit v3 on v2

v3 whole, which is shorter than its diff:
```python
import jax
import jax.numpy as jnp
from jax import lax
from jax.experimental import pallas as pl
from jax.experimental.pallas import tpu as pltpu
from jax.sharding import PartitionSpec as P

MESH = pl.DeviceIdType.MESH
BF, F32 = jnp.bfloat16, jnp.float32
S, C, D, Z = 32, 32, 32, 128
N = 16
L = 4
R = N * L
SCALE = 1.0 / S


def dot(a, b):
    return jnp.dot(a, b, preferred_element_type=F32)


def iota(shape, dim):
    return lax.broadcasted_iota(jnp.int32, shape, dim)


def one_hot(condition):
    return jnp.where(condition, 1.0, 0.0).astype(BF)


def kernel(
    a_hbm, b_hbm, w_hbm, bias_hbm, x_hbm, pair, gl_ref, gr_ref, gw_ref,
    a_own, b_own, w_own, bias, x, xt, wp, wpt, w32, mask, g, o, arep, arept, bp, bpt, b32, bs32,
    gwt, gr, gs32, rows32, fold, gather_s,
    a_all, b_all, w1_out, w1_in, w2_out, w2_in, l_out, l_in, r_out, r_in,
    own_sem, x_sem, send, recv,
):
    row, col = lax.axis_index("row"), lax.axis_index("col")

    def on_col(k):
        return (row, k)

    def on_row(k):
        return (k, col)

    def push(src, dst, which, device):
        pltpu.make_async_remote_copy(
            src_ref=src, dst_ref=dst, send_sem=send.at[which], recv_sem=recv.at[which],
            device_id=device, device_id_type=MESH,
        ).start()

    def others(me, body):
        def step(t, carry):
            body(lax.rem(me + t, N))
            return carry

        lax.fori_loop(1, N, step, 0)

    def wait_all(ref, sem):
        blocks = ref.at[pl.ds(0, N - 1)]
        pltpu.make_async_copy(blocks, blocks, sem).wait()

    A, B, W1, W2, GL, GR = range(6)

    loads = [
        pltpu.make_async_copy(src, dst, own_sem.at[n])
        for n, (src, dst) in enumerate(((a_hbm, a_own), (b_hbm, b_own), (w_hbm, w_own), (bias_hbm, bias)))
    ]
    for load in loads:
        load.start()

    def x_load(q):
        part = pl.ds(q * 16, 16)
        return pltpu.make_async_copy(x_hbm.at[part], x.at[part], x_sem.at[q])

    for q in range(4):
        x_load(q).start()

    barrier = pltpu.get_barrier_semaphore()

    def greet(k, to):
        pl.semaphore_signal(barrier, inc=1, device_id=to(k), device_id_type=MESH)

    others(row, lambda k: greet(k, on_row))
    others(col, lambda k: greet(k, on_col))

    mask[...] = one_hot(iota((256, 256), 0) // 32 == iota((256, 256), 1) // 32)
    m, n = iota((512, 128), 0), iota((512, 128), 1)
    fold[...] = one_hot((m // 128 == n // 32) & (m % 32 == n % 32))
    m, n = iota((16, 128), 0), iota((16, 128), 1)
    gather_s[...] = one_hot((m % 4 == n // 32) & (m // 4 == n % 32 // 8))
    same_block = iota((32, 128), 0) % 4 == iota((32, 128), 1) // 32
    same_dl = iota((128, 256), 0) % 8 == iota((128, 256), 1) // 32

    loads[0].wait()
    loads[1].wait()

    def unfolded(ref):
        parts = []
        for i in range(L):
            tiles = [
                jnp.broadcast_to(ref[pl.ds(i, 1), pl.ds(h * 128, 128)].astype(F32), (4, 128)) for h in range(8)
            ]
            parts.append(jnp.where(same_block, jnp.concatenate(tiles, axis=0), 0.0).astype(BF))
        return jnp.concatenate(parts, axis=1)

    own = dot(jnp.concatenate([unfolded(a_own), unfolded(b_own)], axis=0), fold[...])
    a_all[col] = own[0:32].astype(BF)
    spread_s = one_hot(iota((32, 256), 0) == iota((32, 256), 1) % 32)
    wide = jnp.where(same_dl, dot(own[32:64].T.astype(BF), spread_s), 0.0).astype(BF)
    b_all[row] = dot(gather_s[...], wide).astype(BF)

    loads[2].wait()
    loads[3].wait()
    w32[...] = w_own[...].astype(F32)
    for d in range(D):
        wp[pl.ds(d * C, C), :] = w32[pl.ds(d, C, stride=D), :].astype(BF)
    for q in range(8):
        wpt[:, pl.ds(q * 128, 128)] = wp[pl.ds(q * 128, 128), :].T

    def outer_grad(q):
        x_load(q).wait()
        rows = x[pl.ds(q * 16, 16)].reshape(16 * R, Z)
        part = dot(rows, wpt[...]).astype(BF)
        for dh in range(4):
            g[pl.ds(q * 16, 16), pl.ds(dh * R, R), :] = part[:, dh * 256 : dh * 256 + 256].reshape(16, R, 256)

    def x_transpose(q):
        for h in range(4):
            rows = x[pl.ds(q * 16 + h * 4, 4)].reshape(256, Z)
            xt[q, :, pl.ds(h * 256, 256)] = rows.T

    outer_grad(0)
    outer_grad(1)

    pl.semaphore_wait(barrier, 2 * (N - 1))
    others(row, lambda k: push(b_all.at[row], b_all.at[row], B, on_row(k)))
    others(col, lambda k: push(a_all.at[col], a_all.at[col], A, on_col(k)))

    outer_grad(2)
    outer_grad(3)
    for q in range(4):
        x_transpose(q)
    m, n = iota((128, 1024), 0), iota((128, 1024), 1)
    spread = jnp.where((m // 32 == n // 256) & (m % 32 == n % 32), SCALE, 0.0).astype(BF)

    wait_all(b_all, recv.at[B])
    bs32[...] = b_all[...].astype(F32)
    for q in range(N):
        for dh in range(4):
            b32[pl.ds(dh * R + q * L, L), :] = bs32[q, pl.ds(dh * L, L), :]
    bp[...] = b32[...].astype(BF)
    bpt[...] = b32[...].T.astype(BF)
    wait_all(a_all, recv.at[A])
    arep[...] = dot(a_all[...].reshape(N * S, 128), spread).astype(BF).reshape(N, S, 1024)
    for q in range(4):
        turned = a_all[pl.ds(q * 4, 4)].reshape(128, 128).T
        arept[q] = dot(turned, spread).astype(BF)

    def diagonal(block):
        return jnp.concatenate([block] * 8, axis=0) * mask[...]

    def outer(q, carry):
        for t in range(4):
            for i in range(L):
                rhs = diagonal(arep[q * 4 + t, :, pl.ds(i * 256, 256)])
                o[q * 16 + t * 4 + i] = dot(bp[...], rhs).astype(BF)
        return carry

    lax.fori_loop(0, 4, outer, 0)

    for dh in range(4):
        rows = [o[pl.ds(q * 16, 16), pl.ds(dh * R, R), :].reshape(16 * R, 256) for q in range(4)]
        part = dot(xt[0], rows[0]) + dot(xt[1], rows[1]) + dot(xt[2], rows[2]) + dot(xt[3], rows[3])
        for h in range(2):
            gwt[pl.ds(dh * 256 + h * 128, 128), :] = part[:, h * 128 : h * 128 + 128].T
        for k in (2 * dh, 2 * dh + 1, 2 * dh + 8, 2 * dh + 9):
            for dl in range(4):
                first = (4 * (k % 8) + dl) * C + k // 8
                w1_out[k, pl.ds(dl * 16, 16), :] = gwt[pl.ds(first, 16, stride=2), :].astype(BF)

            @pl.when(k != col)
            def _():
                push(w1_out.at[k], w1_in.at[col], W1, on_col(k))

    w1_in[col] = w1_out[col]

    for q in range(4):
        lhs = jnp.concatenate([g[q * 16 + i] for i in range(16)], axis=1)
        rhs = jnp.concatenate(
            [diagonal(arept[q, pl.ds(i % 4 * 32, 32), pl.ds(i // 4 * 256, 256)]) for i in range(16)], axis=0
        )
        if q == 0:
            gr[...] = dot(lhs, rhs)
        else:
            gr[...] += dot(lhs, rhs)
    for q in range(N):
        for dh in range(4):
            gs32[q, pl.ds(dh * L, L), :] = gr[pl.ds(dh * R + q * L, L), :]
    r_out[...] = gs32[...].astype(BF)
    r_in[row] = r_out[row]
    others(row, lambda k: push(r_out.at[k], r_in.at[row], GR, on_row(k)))

    lane4 = iota((32, 256), 1) % 128 // 32
    lane = iota((32, 128), 1) // 32

    def left_group(q):
        result = jnp.zeros((32, 128), F32)
        for two in range(2):
            i0 = q * L + two * 2
            both = jnp.zeros((32, 256), F32)
            for h in range(2):
                half = pl.ds(h * 128, 128)
                rhs = jnp.concatenate([g[i0, :, half], g[i0 + 1, :, half]], axis=1)
                part = dot(bpt[half, :], rhs)
                kept = part[96:128]
                for dl in range(3):
                    kept = jnp.where(lane4 == dl, part[dl * 32 : dl * 32 + 32], kept)
                both += kept
            for i in range(2):
                one = both[:, i * 128 : i * 128 + 128]
                one = one + pltpu.roll(one, 64, 1)
                one = one + pltpu.roll(one, 32, 1)
                result = jnp.where(lane == two * 2 + i, one, result)
        l_out[q] = result.astype(BF)

    def left_step(u, carry):
        for v in range(8):
            left_group(lax.rem(col + 8 * u + v + 1, N))
        for v in range(8):
            t = 8 * u + v + 1
            q = lax.rem(col + t, N)

            @pl.when(t < N)
            def _():
                push(l_out.at[q], l_in.at[col], GL, on_col(q))

        return carry

    lax.fori_loop(0, 2, left_step, 0)
    l_in[col] = l_out[col]

    wait_all(w1_in, recv.at[W1])
    total = w1_in[0].astype(F32)
    for k in range(1, N):
        total += w1_in[k].astype(F32)
    gwt[pl.ds(0, 64), :] = total
    for k in range(N):
        w2_out[k] = jnp.concatenate([gwt[pl.ds(k, 4, stride=16), :]] * 2, axis=0)
    w2_in[row] = w2_out[row]
    others(row, lambda k: push(w2_out.at[k], w2_in.at[row], W2, on_row(k)))

    for q in range(16):
        lhs = jnp.concatenate(
            [o[pl.ds(q * 4, 4), pl.ds(dh * R, R), :].reshape(4 * R, 256) for dh in range(4)], axis=1
        )
        total = dot(lhs, wp[...]) + bias[...]
        pair[pl.ds(q * 4, 4)] = total.astype(BF).reshape(4, R, Z)

    def folded(block):
        wide = lax.dot_general(block, fold[...], (((1,), (1,)), ((), ())), preferred_element_type=F32)
        kept = jnp.where(jnp.concatenate([same_block] * 4, axis=1), wide, 0.0).astype(BF)
        heads = one_hot(iota((8, 32), 0) == iota((8, 32), 1) // 4)
        tiles = dot(heads, kept)
        for i in range(L):
            for h in range(8):
                rows32[pl.ds(i, 1), pl.ds(h * 128, 128)] = tiles[h : h + 1, i * 128 : i * 128 + 128]
        return rows32[0:4, :].astype(BF)

    wait_all(r_in, recv.at[GR])
    total = r_in[0].astype(F32)
    for k in range(1, N):
        total += r_in[k].astype(F32)
    wide = lax.dot_general(
        gather_s[...], total.astype(BF), (((0,), (0,)), ((), ())), preferred_element_type=F32
    )
    wide = jnp.where(same_dl, wide, 0.0).astype(BF)
    by_s = lax.dot_general(spread_s, wide, (((1,), (1,)), ((), ())), preferred_element_type=F32)
    gr_ref[...] = folded(by_s.astype(BF))

    wait_all(l_in, recv.at[GL])
    total = l_in[0].astype(F32)
    for k in range(1, N):
        total += l_in[k].astype(F32)
    gl_ref[...] = folded((total * SCALE).astype(BF))

    wait_all(w2_in, recv.at[W2])
    total = w2_in[0]
    for k in range(1, N):
        total += w2_in[k]
    gw_ref[...] = total[0:4]

    for ref, which in ((a_all, A), (b_all, B), (w1_in, W1), (w2_in, W2), (l_in, GL), (r_in, GR)):
        wait_all(ref, send.at[which])


def store(pair, gl, gr, gw, pair_hbm, gl_hbm, gr_hbm, gw_hbm, sem):
    copies = [pltpu.make_async_copy(src, dst, sem.at[n]) for n, (src, dst) in enumerate(
        [(pair.at[pl.ds(q * 8, 8)], pair_hbm.at[pl.ds(q * 8, 8)]) for q in range(8)]
        + [(gl, gl_hbm), (gr, gr_hbm), (gw, gw_hbm)])]
    for copy in copies:
        copy.start()
    for copy in copies:
        copy.wait()


def shards(a, b, w, bias, x):
    vmem = pl.BlockSpec(memory_space=pltpu.VMEM)
    hbm = pl.BlockSpec(memory_space=pltpu.HBM)
    v = pltpu.VMEM
    outs = (
        jax.ShapeDtypeStruct((R, R, Z), BF),
        jax.ShapeDtypeStruct((L, S * C), BF),
        jax.ShapeDtypeStruct((L, S * D), BF),
        jax.ShapeDtypeStruct((4, Z), F32),
    )
    results = pl.pallas_call(
        kernel,
        out_shape=outs,
        in_specs=[hbm] * 5,
        out_specs=(vmem,) * 4,
        scratch_shapes=[
            v((L, 1024), BF), v((L, 1024), BF), v((1024, Z), BF), v((1, Z), F32),
            v((R, R, Z), BF), v((4, Z, 1024), BF), v((1024, Z), BF), v((Z, 1024), BF), v((1024, Z), F32),
            v((256, 256), BF), v((R, 256, 256), BF), v((R, 256, 256), BF),
            v((N, S, 1024), BF), v((4, 128, 1024), BF),
            v((256, 256), BF), v((256, 256), BF), v((256, 256), F32), v((N, 16, 256), F32),
            v((1024, Z), F32), v((256, 256), F32), v((N, 16, 256), F32),
            v((8, 1024), F32), v((512, 128), BF), v((16, 128), BF),
            v((N, S, 128), BF), v((N, 16, 256), BF),
            v((N, 64, Z), BF), v((N, 64, Z), BF), v((N, 8, Z), F32), v((N, 8, Z), F32),
            v((N, S, 128), BF), v((N, S, 128), BF), v((N, 16, 256), BF), v((N, 16, 256), BF),
            pltpu.SemaphoreType.DMA((4,)), pltpu.SemaphoreType.DMA((4,)),
            pltpu.SemaphoreType.DMA((6,)), pltpu.SemaphoreType.DMA((6,)),
        ],
        compiler_params=pltpu.CompilerParams(
            collective_id=0, has_side_effects=True, vmem_limit_bytes=48 * 2**20
        ),
        cost_estimate=pl.CostEstimate(
            flops=8_000_000_000, bytes_accessed=3_000_000, transcendentals=0
        ),
    )(*[pltpu.with_memory_space_constraint(t, pltpu.HBM) for t in (a, b, w, bias.reshape(1, Z), x)])
    return pl.pallas_call(
        store,
        out_shape=outs,
        in_specs=[vmem] * 4,
        out_specs=(hbm,) * 4,
        scratch_shapes=[pltpu.SemaphoreType.DMA((11,))],
    )(*results)


def solution(mesh):
    in_specs = (P(("row", "col"), None), P(("col", "row"), None), P(), P(), P("row", "col", None))
    out_specs = (
        P("row", "col", None),
        P(("row", "col"), None),
        P(("col", "row"), None),
        P(("row", "col"), None),
    )
    return jax.shard_map(shards, mesh=mesh, in_specs=in_specs, out_specs=out_specs, check_vma=False)
```

time: 44.1 us -> 42.4 us (0.961)
  local copies, waits for them, and re-layouts: 7.18 us -> 2.72 us
  Pallas kernels: 36.1 us -> 38.9 us
    reshape x10 -> x0, local copies, waits for them, and re-layouts: 3.71 us -> none  [the longest x3 1 us: shards(): gr = gr.reshape(4, L, 8, S).transpose(1, 3, 0, 2).reshape(L, S * D)]
    pallas_call x1 -> x2, Pallas kernels: 36.1 us -> 38.9 us  [the longest x1 36.6 us: shards(): pl.pallas_call(kernel, out_shape=outs, in_specs=[hbm] * 5, out_specs=(vme...]
    unnamed x8, local copies, waits for them, and re-layouts: 3.33 us -> 2.72 us
where the time goes in v3:
time: 42.4 us; the launch traced here: 42.3 us
  Pallas kernels  38.9 us (92%)
  local copies, waits for them, and re-layouts  2.72 us (6%)
  between operations  0.65 us (2%)
    pallas_call x1, Pallas kernels, shards(): pl.pallas_call(kernel, out_shape=outs, in_specs=[hbm] * 5, out_specs=(vme...  36.6 us
    unnamed x8, local copies, waits for them, and re-layouts  2.72 us
    pallas_call x1, Pallas kernels, shards(): pl.pallas_call(store, out_shape=outs, in_specs=[vmem] * 4, out_specs=(hbm...  2.3 us

profile of v3, /device:TPU:1, one launch (start us, length us, event | category | flops | bytes accessed | tf_op | source)
XLA Modules:
  0.0 42.3 jit_solution(7277785702197997373)
XLA Ops:
  0.6 36.6 %shard_map.84 = (bf16[64,64,128]{2,1,0:T(8,128)(2,1)S(1)}, bf16[4,1024]{1,0:T(4,128)(2,1)S(1)}, bf16[4,1024]{1,0:T(4,128)(2,1)S(1)}, f32[4,128]{1,0:T(4,128)S(1)}) custom-call(bf16[4,1024]{1,0:T(4,128)(2,1)} %a_hbm.1, bf16[4,1024]{1,0:T(4,128)(2,1)} %b_hbm.1, bf16[1024,128]{1,0:T(8,128)(2,1)} %w_hbm.1, f32[1,128]{1,0:T(1,128)} %bitcast.1, ...), custom_call_target="tpu_custom_call" | custom-call | flops 8000000000 | bytes 3000000 | tf_op jit(solution)/shard_map/pallas_call | solution.py:315
  37.3 0.0 copy-start
  37.3 1.0 %copy-done = bf16[64,64,128]{2,1,0:T(8,128)(2,1)} copy-done((bf16[64,64,128]{2,1,0:T(8,128)(2,1)}, bf16[64,64,128]{2,1,0:T(8,128)(2,1)S(1)}, u32[]{:S(2)}) %copy-start) | copy-done | bytes 1048600
  38.2 0.0 copy-start.1
  38.2 0.6 %copy-done.1 = bf16[4,1024]{1,0:T(4,128)(2,1)} copy-done((bf16[4,1024]{1,0:T(4,128)(2,1)}, bf16[4,1024]{1,0:T(4,128)(2,1)S(1)}, u32[]{:S(2)}) %copy-start.1) | copy-done | bytes 8216
  38.8 0.0 copy-start.2
  38.8 0.6 %copy-done.2 = bf16[4,1024]{1,0:T(4,128)(2,1)} copy-done((bf16[4,1024]{1,0:T(4,128)(2,1)}, bf16[4,1024]{1,0:T(4,128)(2,1)S(1)}, u32[]{:S(2)}) %copy-start.2) | copy-done | bytes 8216
  39.4 0.0 copy-start.3
  39.4 0.6 %copy-done.3 = f32[4,128]{1,0:T(4,128)} copy-done((f32[4,128]{1,0:T(4,128)}, f32[4,128]{1,0:T(4,128)S(1)}, u32[]{:S(2)}) %copy-start.3) | copy-done | bytes 2072
  40.0 2.3 %shard_map.85 = (bf16[64,64,128]{2,1,0:T(8,128)(2,1)}, bf16[4,1024]{1,0:T(4,128)(2,1)}, bf16[4,1024]{1,0:T(4,128)(2,1)}, f32[4,128]{1,0:T(4,128)}) custom-call(bf16[64,64,128]{2,1,0:T(8,128)(2,1)} %copy-done, bf16[4,1024]{1,0:T(4,128)(2,1)} %copy-done.1, bf16[4,1024]{1,0:T(4,128)(2,1)} %copy-done.2, f32[4,128]{1,0:T(4,128)} %copy-done.3), custom_call_target="tpu_custom_call" | custom-call | tf_op jit(solution)/shard_map/pallas_call | solution.py:341
Async XLA Ops:
  37.3 1.0 %copy-start = (bf16[64,64,128]{2,1,0:T(8,128)(2,1)}, bf16[64,64,128]{2,1,0:T(8,128)(2,1)S(1)}, u32[]{:S(2)}) copy-start(bf16[64,64,128]{2,1,0:T(8,128)(2,1)S(1)} %get-tuple-element.8.pair) | copy-start | bytes 3145732
  38.2 0.6 %copy-start.1 = (bf16[4,1024]{1,0:T(4,128)(2,1)}, bf16[4,1024]{1,0:T(4,128)(2,1)S(1)}, u32[]{:S(2)}) copy-start(bf16[4,1024]{1,0:T(4,128)(2,1)S(1)} %get-tuple-element.9.gl) | copy-start | bytes 24580
  38.8 0.6 %copy-start.2 = (bf16[4,1024]{1,0:T(4,128)(2,1)}, bf16[4,1024]{1,0:T(4,128)(2,1)S(1)}, u32[]{:S(2)}) copy-start(bf16[4,1024]{1,0:T(4,128)(2,1)S(1)} %get-tuple-element.10.gr) | copy-start | bytes 24580
  39.4 0.6 %copy-start.3 = (f32[4,128]{1,0:T(4,128)}, f32[4,128]{1,0:T(4,128)S(1)}, u32[]{:S(2)}) copy-start(f32[4,128]{1,0:T(4,128)S(1)} %get-tuple-element.11.gw) | copy-start | bytes 6148

commit v4 on v3

--- a/solution.py
+++ b/solution.py
@@ -35,6 +35,21 @@
 ):
     row, col = lax.axis_index("row"), lax.axis_index("col")
 
+    y, z = row // 4, lax.rem(row, 4)
+    u, zl, core = col // 4, lax.rem(col // 2, 2), lax.rem(col, 2)
+    around, apart = (0, 1, 2, 1), (0, 2, 4, 2)
+    row_steps = sorted(
+        ((dy, dz) for dy in range(4) for dz in range(4) if dy or dz), key=lambda t: -around[t[0]] - apart[t[1]]
+    )
+    col_steps = sorted(
+        ((dx, dz, dc) for dx in range(4) for dz in range(2) for dc in range(2) if dx or dz or dc),
+        key=lambda t: -around[t[0]] - t[1],
+    )
+    row_peers = [lax.rem(y + dy, 4) * 4 + lax.rem(z + dz, 4) for dy, dz in row_steps]
+    col_peers = [
+        lax.rem(u + dx, 4) * 4 + lax.rem(zl + dz, 2) * 2 + lax.rem(core + dc, 2) for dx, dz, dc in col_steps
+    ]
+
     def on_col(k):
         return (row, k)
 
@@ -47,12 +62,9 @@
             device_id=device, device_id_type=MESH,
         ).start()
 
-    def others(me, body):
-        def step(t, carry):
-            body(lax.rem(me + t, N))
-            return carry
-
-        lax.fori_loop(1, N, step, 0)
+    def others(peers, body):
+        for k in peers:
+            body(k)
 
     def wait_all(ref, sem):
         blocks = ref.at[pl.ds(0, N - 1)]
@@ -79,8 +91,8 @@
     def greet(k, to):
         pl.semaphore_signal(barrier, inc=1, device_id=to(k), device_id_type=MESH)
 
-    others(row, lambda k: greet(k, on_row))
-    others(col, lambda k: greet(k, on_col))
+    others(row_peers, lambda k: greet(k, on_row))
+    others(col_peers, lambda k: greet(k, on_col))
 
     mask[...] = one_hot(iota((256, 256), 0) // 32 == iota((256, 256), 1) // 32)
     m, n = iota((512, 128), 0), iota((512, 128), 1)
@@ -132,8 +144,8 @@
     outer_grad(1)
 
     pl.semaphore_wait(barrier, 2 * (N - 1))
-    others(row, lambda k: push(b_all.at[row], b_all.at[row], B, on_row(k)))
-    others(col, lambda k: push(a_all.at[col], a_all.at[col], A, on_col(k)))
+    others(row_peers, lambda k: push(b_all.at[row], b_all.at[row], B, on_row(k)))
+    others(col_peers, lambda k: push(a_all.at[col], a_all.at[col], A, on_col(k)))
 
     outer_grad(2)
     outer_grad(3)
@@ -142,13 +154,6 @@
     m, n = iota((128, 1024), 0), iota((128, 1024), 1)
     spread = jnp.where((m // 32 == n // 256) & (m % 32 == n % 32), SCALE, 0.0).astype(BF)
 
-    wait_all(b_all, recv.at[B])
-    bs32[...] = b_all[...].astype(F32)
-    for q in range(N):
-        for dh in range(4):
-            b32[pl.ds(dh * R + q * L, L), :] = bs32[q, pl.ds(dh * L, L), :]
-    bp[...] = b32[...].astype(BF)
-    bpt[...] = b32[...].T.astype(BF)
     wait_all(a_all, recv.at[A])
     arep[...] = dot(a_all[...].reshape(N * S, 128), spread).astype(BF).reshape(N, S, 1024)
     for q in range(4):
@@ -157,31 +162,6 @@
 
     def diagonal(block):
         return jnp.concatenate([block] * 8, axis=0) * mask[...]
-
-    def outer(q, carry):
-        for t in range(4):
-            for i in range(L):
-                rhs = diagonal(arep[q * 4 + t, :, pl.ds(i * 256, 256)])
-                o[q * 16 + t * 4 + i] = dot(bp[...], rhs).astype(BF)
-        return carry
-
-    lax.fori_loop(0, 4, outer, 0)
-
-    for dh in range(4):
-        rows = [o[pl.ds(q * 16, 16), pl.ds(dh * R, R), :].reshape(16 * R, 256) for q in range(4)]
-        part = dot(xt[0], rows[0]) + dot(xt[1], rows[1]) + dot(xt[2], rows[2]) + dot(xt[3], rows[3])
-        for h in range(2):
-            gwt[pl.ds(dh * 256 + h * 128, 128), :] = part[:, h * 128 : h * 128 + 128].T
-        for k in (2 * dh, 2 * dh + 1, 2 * dh + 8, 2 * dh + 9):
-            for dl in range(4):
-                first = (4 * (k % 8) + dl) * C + k // 8
-                w1_out[k, pl.ds(dl * 16, 16), :] = gwt[pl.ds(first, 16, stride=2), :].astype(BF)
-
-            @pl.when(k != col)
-            def _():
-                push(w1_out.at[k], w1_in.at[col], W1, on_col(k))
-
-    w1_in[col] = w1_out[col]
 
     for q in range(4):
         lhs = jnp.concatenate([g[q * 16 + i] for i in range(16)], axis=1)
@@ -197,7 +177,45 @@
             gs32[q, pl.ds(dh * L, L), :] = gr[pl.ds(dh * R + q * L, L), :]
     r_out[...] = gs32[...].astype(BF)
     r_in[row] = r_out[row]
-    others(row, lambda k: push(r_out.at[k], r_in.at[row], GR, on_row(k)))
+    others(row_peers, lambda k: push(r_out.at[k], r_in.at[row], GR, on_row(k)))
+
+    wait_all(b_all, recv.at[B])
+    bs32[...] = b_all[...].astype(F32)
+    for q in range(N):
+        for dh in range(4):
+            b32[pl.ds(dh * R + q * L, L), :] = bs32[q, pl.ds(dh * L, L), :]
+    bp[...] = b32[...].astype(BF)
+    bpt[...] = b32[...].T.astype(BF)
+    def outer(q, carry):
+        for t in range(8):
+            for i in range(L):
+                rhs = diagonal(arep[q * 8 + t, :, pl.ds(i * 256, 256)])
+                o[q * 32 + t * 4 + i] = dot(bp[...], rhs).astype(BF)
+        return carry
+
+    lax.fori_loop(0, 2, outer, 0)
+
+    side = lax.rem(u, 2)
+    for sx, sz in ((0, 1), (0, 0), (1, 1), (1, 0)):
+        x1, z1 = lax.rem(side + sx, 2), lax.rem(zl + sz, 2)
+        dh = x1 * 2 + z1
+        rows = [o[pl.ds(q * 16, 16), pl.ds(dh * R, R), :].reshape(16 * R, 256) for q in range(4)]
+        part = dot(xt[0], rows[0]) + dot(xt[1], rows[1]) + dot(xt[2], rows[2]) + dot(xt[3], rows[3])
+        for h in range(2):
+            gwt[pl.ds(h * 128, 128), :] = part[:, h * 128 : h * 128 + 128].T
+        for up in (1, 0):
+            for c1 in range(2):
+                first_x = lax.rem(u + 2 * up, 4) if sx == 0 else x1 + 2 * up
+                k = first_x * 4 + z1 * 2 + c1
+                for dl in range(4):
+                    first = (4 * c1 + dl) * C + first_x // 2
+                    w1_out[k, pl.ds(dl * 16, 16), :] = gwt[pl.ds(first, 16, stride=2), :].astype(BF)
+
+                @pl.when(k != col)
+                def _():
+                    push(w1_out.at[k], w1_in.at[col], W1, on_col(k))
+
+    w1_in[col] = w1_out[col]
 
     lane4 = iota((32, 256), 1) % 128 // 32
     lane = iota((32, 128), 1) // 32
@@ -238,22 +256,27 @@
     lax.fori_loop(0, 2, left_step, 0)
     l_in[col] = l_out[col]
 
+    def pair_blocks(blocks):
+        for q in blocks:
+            lhs = jnp.concatenate(
+                [o[pl.ds(q * 4, 4), pl.ds(dh * R, R), :].reshape(4 * R, 256) for dh in range(4)], axis=1
+            )
+            total = dot(lhs, wp[...]) + bias[...]
+            pair[pl.ds(q * 4, 4)] = total.astype(BF).reshape(4, R, Z)
+
+    pair_blocks(range(8))
+
     wait_all(w1_in, recv.at[W1])
     total = w1_in[0].astype(F32)
     for k in range(1, N):
         total += w1_in[k].astype(F32)
     gwt[pl.ds(0, 64), :] = total
     for k in range(N):
-        w2_out[k] = jnp.concatenate([gwt[pl.ds(k, 4, stride=16), :]] * 2, axis=0)
+        w2_out[k] = gwt[pl.ds(k, 4, stride=16), :]
     w2_in[row] = w2_out[row]
-    others(row, lambda k: push(w2_out.at[k], w2_in.at[row], W2, on_row(k)))
-
-    for q in range(16):
-        lhs = jnp.concatenate(
-            [o[pl.ds(q * 4, 4), pl.ds(dh * R, R), :].reshape(4 * R, 256) for dh in range(4)], axis=1
-        )
-        total = dot(lhs, wp[...]) + bias[...]
-        pair[pl.ds(q * 4, 4)] = total.astype(BF).reshape(4, R, Z)
+    others(row_peers, lambda k: push(w2_out.at[k], w2_in.at[row], W2, on_row(k)))
+
+    pair_blocks(range(8, 16))
 
     def folded(block):
         wide = lax.dot_general(block, fold[...], (((1,), (1,)), ((), ())), preferred_element_type=F32)
@@ -282,14 +305,14 @@
         total += l_in[k].astype(F32)
     gl_ref[...] = folded((total * SCALE).astype(BF))
 
+    for ref, which in ((a_all, A), (b_all, B), (w1_in, W1), (l_in, GL), (r_in, GR), (w2_in, W2)):
+        wait_all(ref, send.at[which])
+
     wait_all(w2_in, recv.at[W2])
     total = w2_in[0]
     for k in range(1, N):
         total += w2_in[k]
-    gw_ref[...] = total[0:4]
-
-    for ref, which in ((a_all, A), (b_all, B), (w1_in, W1), (w2_in, W2), (l_in, GL), (r_in, GR)):
-        wait_all(ref, send.at[which])
+    gw_ref[...] = total
 
 
 def store(pair, gl, gr, gw, pair_hbm, gl_hbm, gr_hbm, gw_hbm, sem):
@@ -323,10 +346,10 @@
             v((256, 256), BF), v((R, 256, 256), BF), v((R, 256, 256), BF),
             v((N, S, 1024), BF), v((4, 128, 1024), BF),
             v((256, 256), BF), v((256, 256), BF), v((256, 256), F32), v((N, 16, 256), F32),
-            v((1024, Z), F32), v((256, 256), F32), v((N, 16, 256), F32),
+            v((256, Z), F32), v((256, 256), F32), v((N, 16, 256), F32),
             v((8, 1024), F32), v((512, 128), BF), v((16, 128), BF),
             v((N, S, 128), BF), v((N, 16, 256), BF),
-            v((N, 64, Z), BF), v((N, 64, Z), BF), v((N, 8, Z), F32), v((N, 8, Z), F32),
+            v((N, 64, Z), BF), v((N, 64, Z), BF), v((N, 4, Z), F32), v((N, 4, Z), F32),
             v((N, S, 128), BF), v((N, S, 128), BF), v((N, 16, 256), BF), v((N, 16, 256), BF),
             pltpu.SemaphoreType.DMA((4,)), pltpu.SemaphoreType.DMA((4,)),
             pltpu.SemaphoreType.DMA((6,)), pltpu.SemaphoreType.DMA((6,)),
@@ -344,7 +367,8 @@
         in_specs=[vmem] * 4,
         out_specs=(hbm,) * 4,
         scratch_shapes=[pltpu.SemaphoreType.DMA((11,))],
-    )(*results)
+        compiler_params=pltpu.CompilerParams(vmem_limit_bytes=2**20),
+    )(*[pltpu.with_memory_space_constraint(t, pltpu.VMEM) for t in results])
 
 
 def solution(mesh):

time: 42.4 us -> 41.3 us (0.974)
  local copies, waits for them, and re-layouts: 2.72 us -> 0 us
  Pallas kernels: 38.9 us -> 40.4 us
    pallas_call x1, Pallas kernels: 36.6 us -> 39.4 us  [shards(): pl.pallas_call(kernel, out_shape=outs, in_specs=[hbm] * 5, out_specs=(vme...]
    unnamed x8 -> x0, local copies, waits for them, and re-layouts: 2.72 us -> none
    pallas_call x1, Pallas kernels: 2.3 us -> 1.06 us  [shards(): pl.pallas_call(store, out_shape=outs, in_specs=[vmem] * 4, out_specs=(hbm...]
where the time goes in v4:
time: 41.3 us; the launch traced here: 41.2 us
  Pallas kernels  40.4 us (98%)
  between operations  0.8 us (2%)
    pallas_call x1, Pallas kernels, shards(): pl.pallas_call(kernel, out_shape=outs, in_specs=[hbm] * 5, out_specs=(vme...  39.4 us
    pallas_call x1, Pallas kernels, shards(): pl.pallas_call(store, out_shape=outs, in_specs=[vmem] * 4, out_specs=(hbm...  1.06 us

profile of v4, /device:TPU:1, one launch (start us, length us, event | category | flops | bytes accessed | tf_op | source)
XLA Modules:
  0.0 41.2 jit_solution(11361276390464049386)
XLA Ops:
  0.6 39.4 %shard_map.84 = (bf16[64,64,128]{2,1,0:T(8,128)(2,1)S(1)}, bf16[4,1024]{1,0:T(4,128)(2,1)S(1)}, bf16[4,1024]{1,0:T(4,128)(2,1)S(1)}, f32[4,128]{1,0:T(4,128)S(1)}) custom-call(bf16[4,1024]{1,0:T(4,128)(2,1)} %a_hbm.1, bf16[4,1024]{1,0:T(4,128)(2,1)} %b_hbm.1, bf16[1024,128]{1,0:T(8,128)(2,1)} %w_hbm.1, f32[1,128]{1,0:T(1,128)} %bitcast.1, ...), custom_call_target="tpu_custom_call" | custom-call | flops 8000000000 | bytes 3000000 | tf_op jit(solution)/shard_map/pallas_call | solution.py:338
  40.0 1.1 %shard_map.85 = (bf16[64,64,128]{2,1,0:T(8,128)(2,1)}, bf16[4,1024]{1,0:T(4,128)(2,1)}, bf16[4,1024]{1,0:T(4,128)(2,1)}, f32[4,128]{1,0:T(4,128)}) custom-call(bf16[64,64,128]{2,1,0:T(8,128)(2,1)S(1)} %get-tuple-element.8.pair, bf16[4,1024]{1,0:T(4,128)(2,1)S(1)} %get-tuple-element.9.gl, bf16[4,1024]{1,0:T(4,128)(2,1)S(1)} %get-tuple-element.10.gr, ...), custom_call_target="tpu_custom_call" | custom-call | tf_op jit(solution)/shard_map/pallas_call | solution.py:364

commit v5 on v4

--- a/solution.py
+++ b/solution.py
@@ -79,20 +79,20 @@
     for load in loads:
         load.start()
 
+    barrier = pltpu.get_barrier_semaphore()
+
+    def greet(k, to):
+        pl.semaphore_signal(barrier, inc=1, device_id=to(k), device_id_type=MESH)
+
+    others(row_peers, lambda k: greet(k, on_row))
+    others(col_peers, lambda k: greet(k, on_col))
+
     def x_load(q):
         part = pl.ds(q * 16, 16)
         return pltpu.make_async_copy(x_hbm.at[part], x.at[part], x_sem.at[q])
 
     for q in range(4):
         x_load(q).start()
-
-    barrier = pltpu.get_barrier_semaphore()
-
-    def greet(k, to):
-        pl.semaphore_signal(barrier, inc=1, device_id=to(k), device_id_type=MESH)
-
-    others(row_peers, lambda k: greet(k, on_row))
-    others(col_peers, lambda k: greet(k, on_col))
 
     mask[...] = one_hot(iota((256, 256), 0) // 32 == iota((256, 256), 1) // 32)
     m, n = iota((512, 128), 0), iota((512, 128), 1)
@@ -120,6 +120,10 @@
     wide = jnp.where(same_dl, dot(own[32:64].T.astype(BF), spread_s), 0.0).astype(BF)
     b_all[row] = dot(gather_s[...], wide).astype(BF)
 
+    pl.semaphore_wait(barrier, 2 * (N - 1))
+    others(row_peers, lambda k: push(b_all.at[row], b_all.at[row], B, on_row(k)))
+    others(col_peers, lambda k: push(a_all.at[col], a_all.at[col], A, on_col(k)))
+
     loads[2].wait()
     loads[3].wait()
     w32[...] = w_own[...].astype(F32)
@@ -140,15 +144,8 @@
             rows = x[pl.ds(q * 16 + h * 4, 4)].reshape(256, Z)
             xt[q, :, pl.ds(h * 256, 256)] = rows.T
 
-    outer_grad(0)
-    outer_grad(1)
-
-    pl.semaphore_wait(barrier, 2 * (N - 1))
-    others(row_peers, lambda k: push(b_all.at[row], b_all.at[row], B, on_row(k)))
-    others(col_peers, lambda k: push(a_all.at[col], a_all.at[col], A, on_col(k)))
-
-    outer_grad(2)
-    outer_grad(3)
+    for q in range(4):
+        outer_grad(q)
     for q in range(4):
         x_transpose(q)
     m, n = iota((128, 1024), 0), iota((128, 1024), 1)
@@ -163,15 +160,19 @@
     def diagonal(block):
         return jnp.concatenate([block] * 8, axis=0) * mask[...]
 
-    for q in range(4):
-        lhs = jnp.concatenate([g[q * 16 + i] for i in range(16)], axis=1)
-        rhs = jnp.concatenate(
-            [diagonal(arept[q, pl.ds(i % 4 * 32, 32), pl.ds(i // 4 * 256, 256)]) for i in range(16)], axis=0
-        )
-        if q == 0:
-            gr[...] = dot(lhs, rhs)
-        else:
+    gr[...] = jnp.zeros_like(gr)
+
+    def right_grad(step, carry):
+        for v in range(2):
+            q = step * 2 + v
+            lhs = jnp.concatenate([g[q * 16 + i] for i in range(16)], axis=1)
+            rhs = jnp.concatenate(
+                [diagonal(arept[q, pl.ds(i % 4 * 32, 32), pl.ds(i // 4 * 256, 256)]) for i in range(16)], axis=0
+            )
             gr[...] += dot(lhs, rhs)
+        return carry
+
+    lax.fori_loop(0, 2, right_grad, 0)
     for q in range(N):
         for dh in range(4):
             gs32[q, pl.ds(dh * L, L), :] = gr[pl.ds(dh * R + q * L, L), :]

time: 41.3 us -> 39.2 us (0.949)
  Pallas kernels: 40.4 us -> 38.3 us
    pallas_call x1, Pallas kernels: 39.4 us -> 37.2 us  [shards(): pl.pallas_call(kernel, out_shape=outs, in_specs=[hbm] * 5, out_specs=(vme...]
where the time goes in v5:
time: 39.2 us; the launch traced here: 39.1 us
  Pallas kernels  38.3 us (98%)
  between operations  0.8 us (2%)
    pallas_call x1, Pallas kernels, shards(): pl.pallas_call(kernel, out_shape=outs, in_specs=[hbm] * 5, out_specs=(vme...  37.2 us
    pallas_call x1, Pallas kernels, shards(): pl.pallas_call(store, out_shape=outs, in_specs=[vmem] * 4, out_specs=(hbm...  1.06 us

profile of v5, /device:TPU:1, one launch (start us, length us, event | category | flops | bytes accessed | tf_op | source)
XLA Modules:
  0.0 39.1 jit_solution(17104950222168032341)
XLA Ops:
  0.6 37.2 %shard_map.84 = (bf16[64,64,128]{2,1,0:T(8,128)(2,1)S(1)}, bf16[4,1024]{1,0:T(4,128)(2,1)S(1)}, bf16[4,1024]{1,0:T(4,128)(2,1)S(1)}, f32[4,128]{1,0:T(4,128)S(1)}) custom-call(bf16[4,1024]{1,0:T(4,128)(2,1)} %a_hbm.1, bf16[4,1024]{1,0:T(4,128)(2,1)} %b_hbm.1, bf16[1024,128]{1,0:T(8,128)(2,1)} %w_hbm.1, f32[1,128]{1,0:T(1,128)} %bitcast.1, ...), custom_call_target="tpu_custom_call" | custom-call | flops 8000000000 | bytes 3000000 | tf_op jit(solution)/shard_map/pallas_call | solution.py:339
  37.9 1.1 %shard_map.85 = (bf16[64,64,128]{2,1,0:T(8,128)(2,1)}, bf16[4,1024]{1,0:T(4,128)(2,1)}, bf16[4,1024]{1,0:T(4,128)(2,1)}, f32[4,128]{1,0:T(4,128)}) custom-call(bf16[64,64,128]{2,1,0:T(8,128)(2,1)S(1)} %get-tuple-element.8.pair, bf16[4,1024]{1,0:T(4,128)(2,1)S(1)} %get-tuple-element.9.gl, bf16[4,1024]{1,0:T(4,128)(2,1)S(1)} %get-tuple-element.10.gr, ...), custom_call_target="tpu_custom_call" | custom-call | tf_op jit(solution)/shard_map/pallas_call | solution.py:365

commit v6 on v5

--- a/solution.py
+++ b/solution.py
@@ -121,8 +121,9 @@
     b_all[row] = dot(gather_s[...], wide).astype(BF)
 
     pl.semaphore_wait(barrier, 2 * (N - 1))
+    others(col_peers[:6], lambda k: push(a_all.at[col], a_all.at[col], A, on_col(k)))
     others(row_peers, lambda k: push(b_all.at[row], b_all.at[row], B, on_row(k)))
-    others(col_peers, lambda k: push(a_all.at[col], a_all.at[col], A, on_col(k)))
+    others(col_peers[6:], lambda k: push(a_all.at[col], a_all.at[col], A, on_col(k)))
 
     loads[2].wait()
     loads[3].wait()
@@ -159,26 +160,6 @@
 
     def diagonal(block):
         return jnp.concatenate([block] * 8, axis=0) * mask[...]
-
-    gr[...] = jnp.zeros_like(gr)
-
-    def right_grad(step, carry):
-        for v in range(2):
-            q = step * 2 + v
-            lhs = jnp.concatenate([g[q * 16 + i] for i in range(16)], axis=1)
-            rhs = jnp.concatenate(
-                [diagonal(arept[q, pl.ds(i % 4 * 32, 32), pl.ds(i // 4 * 256, 256)]) for i in range(16)], axis=0
-            )
-            gr[...] += dot(lhs, rhs)
-        return carry
-
-    lax.fori_loop(0, 2, right_grad, 0)
-    for q in range(N):
-        for dh in range(4):
-            gs32[q, pl.ds(dh * L, L), :] = gr[pl.ds(dh * R + q * L, L), :]
-    r_out[...] = gs32[...].astype(BF)
-    r_in[row] = r_out[row]
-    others(row_peers, lambda k: push(r_out.at[k], r_in.at[row], GR, on_row(k)))
 
     wait_all(b_all, recv.at[B])
     bs32[...] = b_all[...].astype(F32)
@@ -217,6 +198,26 @@
                     push(w1_out.at[k], w1_in.at[col], W1, on_col(k))
 
     w1_in[col] = w1_out[col]
+
+    gr[...] = jnp.zeros_like(gr)
+
+    def right_grad(step, carry):
+        for v in range(2):
+            q = step * 2 + v
+            lhs = jnp.concatenate([g[q * 16 + i] for i in range(16)], axis=1)
+            rhs = jnp.concatenate(
+                [diagonal(arept[q, pl.ds(i % 4 * 32, 32), pl.ds(i // 4 * 256, 256)]) for i in range(16)], axis=0
+            )
+            gr[...] += dot(lhs, rhs)
+        return carry
+
+    lax.fori_loop(0, 2, right_grad, 0)
+    for q in range(N):
+        for dh in range(4):
+            gs32[q, pl.ds(dh * L, L), :] = gr[pl.ds(dh * R + q * L, L), :]
+    r_out[...] = gs32[...].astype(BF)
+    r_in[row] = r_out[row]
+    others(row_peers, lambda k: push(r_out.at[k], r_in.at[row], GR, on_row(k)))
 
     lane4 = iota((32, 256), 1) % 128 // 32
     lane = iota((32, 128), 1) // 32
@@ -257,16 +258,6 @@
     lax.fori_loop(0, 2, left_step, 0)
     l_in[col] = l_out[col]
 
-    def pair_blocks(blocks):
-        for q in blocks:
-            lhs = jnp.concatenate(
-                [o[pl.ds(q * 4, 4), pl.ds(dh * R, R), :].reshape(4 * R, 256) for dh in range(4)], axis=1
-            )
-            total = dot(lhs, wp[...]) + bias[...]
-            pair[pl.ds(q * 4, 4)] = total.astype(BF).reshape(4, R, Z)
-
-    pair_blocks(range(8))
-
     wait_all(w1_in, recv.at[W1])
     total = w1_in[0].astype(F32)
     for k in range(1, N):
@@ -277,7 +268,13 @@
     w2_in[row] = w2_out[row]
     others(row_peers, lambda k: push(w2_out.at[k], w2_in.at[row], W2, on_row(k)))
 
-    pair_blocks(range(8, 16))
+    for q in range(16):
+        lhs = jnp.concatenate(
+            [o[pl.ds(q * 4, 4), pl.ds(dh * R, R), :].reshape(4 * R, 256) for dh in range(4)], axis=1
+        )
+        total = dot(lhs, wp[...]) + bias[...]
+        pair[pl.ds(q * 4, 4)] = total.astype(BF).reshape(4, R, Z)
+
 
     def folded(block):
         wide = lax.dot_general(block, fold[...], (((1,), (1,)), ((), ())), preferred_element_type=F32)

time: 39.2 us -> 36.7 us (0.936)
  Pallas kernels: 38.3 us -> 35.9 us
    pallas_call x1, Pallas kernels: 37.2 us -> 34.9 us  [shards(): pl.pallas_call(kernel, out_shape=outs, in_specs=[hbm] * 5, out_specs=(vme...]
where the time goes in v6:
time: 36.7 us; the launch traced here: 36.6 us
  Pallas kernels  35.9 us (98%)
  between operations  0.64 us (2%)
    pallas_call x1, Pallas kernels, shards(): pl.pallas_call(kernel, out_shape=outs, in_specs=[hbm] * 5, out_specs=(vme...  34.9 us
    pallas_call x1, Pallas kernels, shards(): pl.pallas_call(store, out_shape=outs, in_specs=[vmem] * 4, out_specs=(hbm...  1.06 us

profile of v6, /device:TPU:1, one launch (start us, length us, event | category | flops | bytes accessed | tf_op | source)
XLA Modules:
  0.0 36.6 jit_solution(7964741254986179919)
XLA Ops:
  0.6 34.9 %shard_map.84 = (bf16[64,64,128]{2,1,0:T(8,128)(2,1)S(1)}, bf16[4,1024]{1,0:T(4,128)(2,1)S(1)}, bf16[4,1024]{1,0:T(4,128)(2,1)S(1)}, f32[4,128]{1,0:T(4,128)S(1)}) custom-call(bf16[4,1024]{1,0:T(4,128)(2,1)} %a_hbm.1, bf16[4,1024]{1,0:T(4,128)(2,1)} %b_hbm.1, bf16[1024,128]{1,0:T(8,128)(2,1)} %w_hbm.1, f32[1,128]{1,0:T(1,128)} %bitcast.1, ...), custom_call_target="tpu_custom_call" | custom-call | flops 8000000000 | bytes 3000000 | tf_op jit(solution)/shard_map/pallas_call | solution.py:336
  35.5 1.1 %shard_map.85 = (bf16[64,64,128]{2,1,0:T(8,128)(2,1)}, bf16[4,1024]{1,0:T(4,128)(2,1)}, bf16[4,1024]{1,0:T(4,128)(2,1)}, f32[4,128]{1,0:T(4,128)}) custom-call(bf16[64,64,128]{2,1,0:T(8,128)(2,1)S(1)} %get-tuple-element.8.pair, bf16[4,1024]{1,0:T(4,128)(2,1)S(1)} %get-tuple-element.9.gl, bf16[4,1024]{1,0:T(4,128)(2,1)S(1)} %get-tuple-element.10.gr, ...), custom_call_target="tpu_custom_call" | custom-call | tf_op jit(solution)/shard_map/pallas_call | solution.py:362

commit v7 on v6

--- a/solution.py
+++ b/solution.py
@@ -121,9 +121,8 @@
     b_all[row] = dot(gather_s[...], wide).astype(BF)
 
     pl.semaphore_wait(barrier, 2 * (N - 1))
-    others(col_peers[:6], lambda k: push(a_all.at[col], a_all.at[col], A, on_col(k)))
+    others(col_peers, lambda k: push(a_all.at[col], a_all.at[col], A, on_col(k)))
     others(row_peers, lambda k: push(b_all.at[row], b_all.at[row], B, on_row(k)))
-    others(col_peers[6:], lambda k: push(a_all.at[col], a_all.at[col], A, on_col(k)))
 
     loads[2].wait()
     loads[3].wait()
@@ -242,21 +241,12 @@
                 result = jnp.where(lane == two * 2 + i, one, result)
         l_out[q] = result.astype(BF)
 
-    def left_step(u, carry):
+    def left_step(step, carry):
         for v in range(8):
-            left_group(lax.rem(col + 8 * u + v + 1, N))
-        for v in range(8):
-            t = 8 * u + v + 1
-            q = lax.rem(col + t, N)
-
-            @pl.when(t < N)
-            def _():
-                push(l_out.at[q], l_in.at[col], GL, on_col(q))
-
+            left_group(step * 8 + v)
         return carry
 
     lax.fori_loop(0, 2, left_step, 0)
-    l_in[col] = l_out[col]
 
     wait_all(w1_in, recv.at[W1])
     total = w1_in[0].astype(F32)
@@ -267,6 +257,8 @@
         w2_out[k] = gwt[pl.ds(k, 4, stride=16), :]
     w2_in[row] = w2_out[row]
     others(row_peers, lambda k: push(w2_out.at[k], w2_in.at[row], W2, on_row(k)))
+    l_in[col] = l_out[col]
+    others(col_peers, lambda k: push(l_out.at[k], l_in.at[col], GL, on_col(k)))
 
     for q in range(16):
         lhs = jnp.concatenate(
@@ -274,7 +266,6 @@
         )
         total = dot(lhs, wp[...]) + bias[...]
         pair[pl.ds(q * 4, 4)] = total.astype(BF).reshape(4, R, Z)
-
 
     def folded(block):
         wide = lax.dot_general(block, fold[...], (((1,), (1,)), ((), ())), preferred_element_type=F32)
@@ -315,7 +306,7 @@
 
 def store(pair, gl, gr, gw, pair_hbm, gl_hbm, gr_hbm, gw_hbm, sem):
     copies = [pltpu.make_async_copy(src, dst, sem.at[n]) for n, (src, dst) in enumerate(
-        [(pair.at[pl.ds(q * 8, 8)], pair_hbm.at[pl.ds(q * 8, 8)]) for q in range(8)]
+        [(pair.at[pl.ds(q * 32, 32)], pair_hbm.at[pl.ds(q * 32, 32)]) for q in range(2)]
         + [(gl, gl_hbm), (gr, gr_hbm), (gw, gw_hbm)])]
     for copy in copies:
         copy.start()
@@ -364,7 +355,7 @@
         out_shape=outs,
         in_specs=[vmem] * 4,
         out_specs=(hbm,) * 4,
-        scratch_shapes=[pltpu.SemaphoreType.DMA((11,))],
+        scratch_shapes=[pltpu.SemaphoreType.DMA((5,))],
         compiler_params=pltpu.CompilerParams(vmem_limit_bytes=2**20),
     )(*[pltpu.with_memory_space_constraint(t, pltpu.VMEM) for t in results])
 

time: 36.7 us -> 36.8 us (level)
  no operation moved by 1% of the time
where the time goes in v7:
time: 36.8 us; the launch traced here: 36.6 us
  Pallas kernels  36 us (98%)
  between operations  0.64 us (2%)
    pallas_call x1, Pallas kernels, shards(): pl.pallas_call(kernel, out_shape=outs, in_specs=[hbm] * 5, out_specs=(vme...  35 us
    pallas_call x1, Pallas kernels, shards(): pl.pallas_call(store, out_shape=outs, in_specs=[vmem] * 4, out_specs=(hbm...  1.02 us

profile of v7, /device:TPU:1, one launch (start us, length us, event | category | flops | bytes accessed | tf_op | source)
XLA Modules:
  0.0 36.6 jit_solution(5027187727691607753)
XLA Ops:
  0.6 35.0 %shard_map.84 = (bf16[64,64,128]{2,1,0:T(8,128)(2,1)S(1)}, bf16[4,1024]{1,0:T(4,128)(2,1)S(1)}, bf16[4,1024]{1,0:T(4,128)(2,1)S(1)}, f32[4,128]{1,0:T(4,128)S(1)}) custom-call(bf16[4,1024]{1,0:T(4,128)(2,1)} %a_hbm.1, bf16[4,1024]{1,0:T(4,128)(2,1)} %b_hbm.1, bf16[1024,128]{1,0:T(8,128)(2,1)} %w_hbm.1, f32[1,128]{1,0:T(1,128)} %bitcast.1, ...), custom_call_target="tpu_custom_call" | custom-call | flops 8000000000 | bytes 3000000 | tf_op jit(solution)/shard_map/pallas_call | solution.py:327
  35.6 1.0 %shard_map.85 = (bf16[64,64,128]{2,1,0:T(8,128)(2,1)}, bf16[4,1024]{1,0:T(4,128)(2,1)}, bf16[4,1024]{1,0:T(4,128)(2,1)}, f32[4,128]{1,0:T(4,128)}) custom-call(bf16[64,64,128]{2,1,0:T(8,128)(2,1)S(1)} %get-tuple-element.8.pair, bf16[4,1024]{1,0:T(4,128)(2,1)S(1)} %get-tuple-element.9.gl, bf16[4,1024]{1,0:T(4,128)(2,1)S(1)} %get-tuple-element.10.gr, ...), custom_call_target="tpu_custom_call" | custom-call | tf_op jit(solution)/shard_map/pallas_call | solution.py:353
